TPU v7x, 512 devices: a whole 4x4x16 slice. The times are simulated.
512 devices in a mesh: crop: 16 (over y, x_lo, core), res: 32 (over z, x_hi).
Axes of the slice: x: 4 (x_hi: 2, x_lo: 2; x = x_hi * 2 + x_lo), y: 4, z: 16, core: 2. Of those that a mesh axis runs over, the one named last changes fastest.
Arguments:
- alignment: bfloat16 [2048, 64, 256], P('crop', 'res'), parts along dimension 0, may hold values from -6 to 6
- pair_features: bfloat16 [64, 1024, 128], P('res', 'crop'), parts along dimension 1, may hold values from -6 to 6
- pair_cotangent: bfloat16 [64, 1024, 128], P('res', 'crop'), parts along dimension 1, may hold values from -6 to 6
- outer_weight: bfloat16 [256, 64], replicated, may hold values from -1 to 1
- mean_weight: bfloat16 [1024, 128], replicated, may hold values from -0.1875 to 0.1875
- triangle_weight: bfloat16 [2, 128, 512], replicated, may hold values from -0.5 to 0.5
- gating_weight: bfloat16 [2, 128, 128], replicated, may hold values from -0.5 to 0.5
- mixing_weight: bfloat16 [2, 128, 128], replicated, may hold values from -0.5 to 0.5
Outputs:
- updated_pair: bfloat16 [64, 1024, 128], P('res', 'crop'), parts along dimension 1
- alignment_gradient: float32 [2048, 64, 256], P('crop', 'res'), parts along dimension 0
- pair_gradient: float32 [64, 1024, 128], P('res', 'crop'), parts along dimension 1
- outer_gradient: float32 [4096, 64], P('crop'), parts along dimension 0
- mean_gradient: float32 [16384, 128], P('crop'), parts along dimension 0
- triangle_gradient: float32 [32, 128, 512], P('crop'), parts along dimension 0
- gating_gradient: float32 [32, 128, 128], P('crop'), parts along dimension 0
- mixing_gradient: float32 [32, 128, 128], P('crop'), parts along dimension 0
There are 16 independent parts, one for each index of `crop`. A program takes and returns all parts, laid end to end along the dimension named above; an argument that names none is the same for every part. Nothing has to cross between parts.
All inputs are finite; a program needn't handle non-finite values.
Results may differ from a plain program's by a relative error of at most 0.035.
Values may be sent and summed in bfloat16 or wider, within the bound.
A program may use at most 64 MiB of HBM per device.

v0:
```python
import jax
import jax.numpy as jnp
from jax import lax
from jax.sharding import PartitionSpec as P

EPS = 1e-05


def normalize(values):
    center = jnp.mean(values, axis=-1, keepdims=True)
    shifted = values - center
    inverse = lax.rsqrt(jnp.mean(shifted * shifted, axis=-1, keepdims=True) + EPS)
    return (shifted * inverse, inverse)


def norm_back(normed, inverse, upstream):
    mean_upstream = jnp.mean(upstream, axis=-1, keepdims=True)
    mean_product = jnp.mean(upstream * normed, axis=-1, keepdims=True)
    return inverse * (upstream - mean_upstream - normed * mean_product)


def project(values, weight):
    columns = values.shape[-1]
    flattened = jnp.dot(values.reshape(-1, columns), weight, preferred_element_type=jnp.float32)
    return flattened.reshape(values.shape[:-1] + (weight.shape[1],))


def back_project(upstream, weight):
    columns = upstream.shape[-1]
    flattened = jnp.dot(upstream.reshape(-1, columns), weight.T, preferred_element_type=jnp.float32)
    return flattened.reshape(upstream.shape[:-1] + (weight.shape[0],))


def weight_gradient(values, upstream):
    flat_values = values.reshape(-1, values.shape[-1])
    flat_upstream = upstream.reshape(-1, upstream.shape[-1])
    return jnp.dot(flat_values.T, flat_upstream, preferred_element_type=jnp.float32)


def triangle_head(pair_block, project_weight, gate_weight):
    normed, inverse = normalize(pair_block.astype(jnp.float32))
    normed_half = normed.astype(jnp.bfloat16)
    projected = project(normed_half, project_weight)
    quarter = project_weight.shape[1] // 4
    linear_left = projected[..., :quarter]
    switch_left = jax.nn.sigmoid(projected[..., quarter : 2 * quarter])
    linear_right = projected[..., 2 * quarter : 3 * quarter]
    switch_right = jax.nn.sigmoid(projected[..., 3 * quarter :])
    left_factor = (switch_left * linear_left).astype(jnp.bfloat16)
    right_factor = (switch_right * linear_right).astype(jnp.bfloat16)
    gating = jax.nn.sigmoid(project(normed_half, gate_weight))
    saved = (normed, inverse, normed_half, linear_left, switch_left, linear_right, switch_right)
    return (left_factor, right_factor, gating, saved)


def triangle_tail(pair_block, mixed, gating, mixing):
    mixed_norm, mixed_inverse = normalize(mixed)
    mixed_half = mixed_norm.astype(jnp.bfloat16)
    update = project(mixed_half, mixing)
    updated = (pair_block.astype(jnp.float32) + gating * update).astype(jnp.bfloat16)
    return (updated, (mixed_norm, mixed_inverse, mixed_half, update))


def tail_backward(upstream, gating, saved, mixing):
    mixed_norm, mixed_inverse, mixed_half, update = saved
    update_gradient = (upstream * gating).astype(jnp.bfloat16)
    logit_gradient = (upstream * update * gating * (1.0 - gating)).astype(jnp.bfloat16)
    mixing_grads = weight_gradient(mixed_half, update_gradient)
    mixed_gradient = norm_back(
        mixed_norm, mixed_inverse, back_project(update_gradient, mixing)
    ).astype(jnp.bfloat16)
    return (mixed_gradient, logit_gradient, mixing_grads)


def head_backward(
    upstream, saved, left_gradient, right_gradient, logit_gradient, project_weight, gate_weight
):
    normed, inverse, normed_half, linear_left, switch_left, linear_right, switch_right = saved
    left_wide = left_gradient.astype(jnp.float32)
    right_wide = right_gradient.astype(jnp.float32)
    quarter_gradient = jnp.concatenate(
        [
            left_wide * switch_left,
            left_wide * linear_left * switch_left * (1.0 - switch_left),
            right_wide * switch_right,
            right_wide * linear_right * switch_right * (1.0 - switch_right),
        ],
        axis=-1,
    ).astype(jnp.bfloat16)
    project_grads = weight_gradient(normed_half, quarter_gradient)
    gate_grads = weight_gradient(normed_half, logit_gradient)
    normed_gradient = back_project(quarter_gradient, project_weight) + back_project(
        logit_gradient, gate_weight
    )
    return (upstream + norm_back(normed, inverse, normed_gradient), project_grads, gate_grads)


def on_device(
    alignment,
    pair_features,
    pair_cotangent,
    outer_weight,
    mean_weight,
    triangle_weight,
    gating_weight,
    mixing_weight,
):
    sequences = alignment.shape[0]
    channels = outer_weight.shape[1] // 2
    local_rows = pair_features.shape[0]
    residues = pair_features.shape[1]
    aligned_norm, aligned_inverse = normalize(alignment.astype(jnp.float32))
    aligned_half = aligned_norm.astype(jnp.bfloat16)
    projected = project(aligned_half, outer_weight).astype(jnp.bfloat16)
    outer_left = projected[..., :channels]
    right_local = projected[..., channels:]
    outer_right = lax.all_gather(right_local, "res", axis=1, tiled=True)
    outer_mean = (
        (
            jnp.einsum("sia,sjb->ijab", outer_left, outer_right, preferred_element_type=jnp.float32)
            / sequences
        )
        .reshape(local_rows, residues, channels * channels)
        .astype(jnp.bfloat16)
    )
    first_pair = (pair_features.astype(jnp.float32) + project(outer_mean, mean_weight)).astype(
        jnp.bfloat16
    )
    first_left, first_right, first_gating, first_head = triangle_head(
        first_pair, triangle_weight[0], gating_weight[0]
    )
    first_right_all = lax.all_gather(first_right, "res", axis=0, tiled=True)
    first_mixed = jnp.einsum(
        "ikc,jkc->ijc", first_left, first_right_all, preferred_element_type=jnp.float32
    )
    second_pair, first_tail = triangle_tail(first_pair, first_mixed, first_gating, mixing_weight[0])
    column_pair = lax.all_to_all(second_pair, "res", split_axis=1, concat_axis=0, tiled=True)
    column_left, column_right, column_gating, column_head = triangle_head(
        column_pair, triangle_weight[1], gating_weight[1]
    )
    left_all = lax.all_gather(column_left, "res", axis=1, tiled=True)
    column_mixed = jnp.einsum(
        "kic,kjc->ijc", left_all, column_right, preferred_element_type=jnp.float32
    )
    column_updated, column_tail = triangle_tail(
        column_pair, column_mixed, column_gating, mixing_weight[1]
    )
    updated_pair = lax.all_to_all(column_updated, "res", split_axis=0, concat_axis=1, tiled=True)
    column_upstream = lax.all_to_all(
        pair_cotangent, "res", split_axis=1, concat_axis=0, tiled=True
    ).astype(jnp.float32)
    mixed_gradient, logit_gradient, second_mixing = tail_backward(
        column_upstream, column_gating, column_tail, mixing_weight[1]
    )
    right_gradient = jnp.einsum(
        "ijc,kic->kjc", mixed_gradient, left_all, preferred_element_type=jnp.float32
    ).astype(jnp.bfloat16)
    gradient_by_rows = lax.all_to_all(
        mixed_gradient, "res", split_axis=0, concat_axis=1, tiled=True
    )
    block = gradient_by_rows
    left_gradient = jnp.einsum(
        "ijc,kjc->kic",
        block,
        lax.all_gather(column_right, "res", axis=1, tiled=True),
        preferred_element_type=jnp.float32,
    ).astype(jnp.bfloat16)
    column_gradient, second_project, second_gate = head_backward(
        column_upstream,
        column_head,
        left_gradient,
        right_gradient,
        logit_gradient,
        triangle_weight[1],
        gating_weight[1],
    )
    second_gradient = lax.all_to_all(
        column_gradient.astype(jnp.bfloat16), "res", split_axis=0, concat_axis=1, tiled=True
    ).astype(column_gradient.dtype)
    mixed_gradient, logit_gradient, first_mixing = tail_backward(
        second_gradient, first_gating, first_tail, mixing_weight[0]
    )
    left_gradient = jnp.einsum(
        "ijc,jkc->ikc", mixed_gradient, first_right_all, preferred_element_type=jnp.float32
    ).astype(jnp.bfloat16)
    gradient_by_columns = lax.all_to_all(
        mixed_gradient, "res", split_axis=1, concat_axis=0, tiled=True
    )
    block = gradient_by_columns
    right_gradient = jnp.einsum(
        "ijc,ikc->jkc",
        block,
        lax.all_gather(first_left, "res", axis=0, tiled=True),
        preferred_element_type=jnp.float32,
    ).astype(jnp.bfloat16)
    first_gradient, first_project, first_gate = head_backward(
        second_gradient,
        first_head,
        left_gradient,
        right_gradient,
        logit_gradient,
        triangle_weight[0],
        gating_weight[0],
    )
    mean_cotangent = first_gradient.astype(jnp.bfloat16)
    mean_gradient = weight_gradient(outer_mean, mean_cotangent)
    outer_cotangent = (
        (back_project(mean_cotangent, mean_weight) / sequences)
        .astype(jnp.bfloat16)
        .reshape(local_rows, residues, channels, channels)
    )
    outer_left_gradient = jnp.einsum(
        "ijab,sjb->sia", outer_cotangent, outer_right, preferred_element_type=jnp.float32
    )
    block = outer_cotangent
    outer_right_gradient = jnp.swapaxes(
        lax.psum_scatter(
            jnp.einsum(
                "ijab,sia->jsb", block, outer_left, preferred_element_type=jnp.float32
            ).astype(jnp.bfloat16),
            "res",
            scatter_dimension=0,
            tiled=True,
        ).astype(jnp.float32),
        0,
        1,
    )
    projection_gradient = jnp.concatenate(
        [outer_left_gradient, outer_right_gradient], axis=-1
    ).astype(jnp.bfloat16)
    outer_gradient = weight_gradient(aligned_half, projection_gradient)
    alignment_gradient = norm_back(
        aligned_norm, aligned_inverse, back_project(projection_gradient, outer_weight)
    )
    project_stack = jnp.stack([first_project, second_project])
    gate_stack = jnp.stack([first_gate, second_gate])
    mixing_stack = jnp.stack([first_mixing, second_mixing])
    outer_gradient, mean_gradient, project_stack, gate_stack, mixing_stack = (
        lax.psum(outer_gradient.astype(jnp.bfloat16), "res").astype(jnp.float32),
        lax.psum(mean_gradient.astype(jnp.bfloat16), "res").astype(jnp.float32),
        lax.psum(project_stack.astype(jnp.bfloat16), "res").astype(jnp.float32),
        lax.psum(gate_stack.astype(jnp.bfloat16), "res").astype(jnp.float32),
        lax.psum(mixing_stack.astype(jnp.bfloat16), "res").astype(jnp.float32),
    )
    return (
        updated_pair,
        alignment_gradient,
        first_gradient,
        outer_gradient,
        mean_gradient,
        project_stack,
        gate_stack,
        mixing_stack,
    )


def solution(mesh):
    in_specs = (
        P("crop", "res", None),
        P("res", "crop", None),
        P("res", "crop", None),
        P(),
        P(),
        P(),
        P(),
        P(),
    )
    out_specs = (
        P("res", "crop", None),
        P("crop", "res", None),
        P("res", "crop", None),
        P("crop", None),
        P("crop", None),
        P("crop", None, None),
        P("crop", None, None),
        P("crop", None, None),
    )
    return jax.shard_map(
        on_device, mesh=mesh, in_specs=in_specs, out_specs=out_specs, check_vma=False
    )
```

profile of v0, /device:TPU:24, one launch (start us, length us, event | category | flops | bytes accessed | tf_op | source)
XLA Modules:
  0.0 1825.8 jit_solution(1324284297085033108)
XLA Ops:
  11.1 85.4 %all_gather.15 = bf16[128,64,32]{0,2,1:T(8,128)(2,1)S(1)} all-gather(bf16[128,2,32]{0,2,1:T(8,128)(2,1)S(1)} %slice.70), channel_id=1, replica_groups=mesh['crop'=16,'res'=32] {'res'}, dimensions={1}, use_global_device_ids=true | all-gather | bytes 540672 | tf_op jit(solution)/shard_map/all_gather | solution.py:117
  97.0 1.6 copy.194
  102.6 134.7 %all-gather.5.cloned.1.call-done = bf16[64,64,128]{2,1,0:T(8,128)(2,1)} async-done(((bf16[2,64,128]{2,1,0:T(8,128)(2,1)}), bf16[64,64,128]{2,1,0:T(8,128)(2,1)}) %all-gather.5.cloned.1.call-update) | async-done | bytes 1048592 | tf_op jit(solution)/shard_map/all_gather | solution.py:132
  237.2 3.9 copy.196
  241.2 1.8 fusion.137
  245.3 1.6 add_convert_fusion.2
  247.0 22.2 %all_to_all.81 = bf16[2,64,128]{2,0,1:T(2,128)(2,1)S(1)} all-to-all(bf16[2,64,128]{2,0,1:T(2,128)(2,1)S(1)} %copy.199), channel_id=1, replica_groups=mesh['crop'=16,'res'=32] {'res'}, dimensions={1} | all-to-all | bytes 65536 | tf_op jit(solution)/shard_map/all_to_all | solution.py:137
  270.6 1.4 copy.202
  280.1 17.8 all_to_all.82
  298.5 79.6 %all-gather.11.cloned.1.call-done = bf16[64,64,128]{2,1,0:T(8,128)(2,1)} async-done(((bf16[2,64,128]{2,1,0:T(8,128)(2,1)}), bf16[64,64,128]{2,1,0:T(8,128)(2,1)}) %all-gather.11.cloned.1.call-update) | async-done | bytes 1048592 | tf_op jit(solution)/shard_map/all_gather | solution.py:193
  378.1 4.7 copy.233
  383.5 1.4 rsqrt.49
  385.0 1.4 div.113
  387.3 131.7 %all-gather.7.cloned.1.call-done = bf16[64,64,128]{2,0,1:T(8,128)(2,1)} async-done(((bf16[64,2,128]{2,0,1:T(8,128)(2,1)}), bf16[64,64,128]{2,0,1:T(8,128)(2,1)}) %all-gather.7.cloned.1.call-update) | async-done | bytes 1048592 | tf_op jit(solution)/shard_map/all_gather | solution.py:141
  519.0 4.7 copy.208
  523.7 3.4 fusion.138
  529.4 1.7 multiply_convert_fusion.4
  533.6 1.5 copy.222
  536.5 7.7 all-to-all-start.3
  544.1 2.9 fusion.140
  547.0 1.6 copy.223
  548.6 110.7 %all-gather.9.cloned.1.call-done = bf16[64,64,128]{2,0,1:T(8,128)(2,1)} async-done(((bf16[64,2,128]{2,0,1:T(8,128)(2,1)}), bf16[64,64,128]{2,0,1:T(8,128)(2,1)}) %all-gather.9.cloned.1.call-update) | async-done | bytes 1048592 | tf_op jit(solution)/shard_map/all_gather | solution.py:165
  659.3 4.7 copy.218
  664.0 1.6 fusion.22
  667.2 2.9 fusion.139
  670.1 1.6 copy.220
  676.7 7.5 all-to-all-start.4
  684.2 1.7 fusion.24
  685.9 1.8 fusion.7
  687.8 11.3 all-to-all-done.4
  699.9 1.5 multiply_convert_fusion.1
  704.8 1.5 copy.228
  706.3 1.6 fusion.25
  707.9 3.9 all-to-all-start.5
  711.8 2.1 fusion.141
  715.6 1.4 pad_maximum_fusion.3
  717.0 9.6 all-to-all-done.5
  726.8 2.3 fusion.142
  732.6 1.6 copy.245
  735.5 19.7 %all_to_all.83 = bf16[64,2,128]{2,1,0:T(2,128)(2,1)S(1)} all-to-all(bf16[64,2,128]{2,1,0:T(2,128)(2,1)S(1)} %copy.210), channel_id=1, replica_groups=mesh['crop'=16,'res'=32] {'res'}, dimensions={0} | all-to-all | bytes 65536 | tf_op jit(solution)/shard_map/all_to_all | solution.py:148
  755.9 1.5 copy.237
  757.8 274.2 %all-reduce.3.cloned.1.call-done = (bf16[1024,128]{1,0:T(8,128)(2,1)}, bf16[2,128,512]{2,1,0:T(8,128)(2,1)}, bf16[2,128,128]{2,1,0:T(8,128)(2,1)}, bf16[2,128,128]{2,1,0:T(8,128)(2,1)}) async-done(((bf16[1024,128]{1,0:T(8,128)(2,1)}, bf16[2,128,512]{2,1,0:T(8,128)(2,1)}, bf16[2,128,128]{2,1,0:T(8,128)(2,1)}, bf16[2,128,128]{2,1,0:T(8,128)(2,1)}), (bf16[1024,128]{1,0:T(8,128)(2,1)}, ...) | async-done | bytes 655376 | tf_op jit(solution)/shard_map/psum | solution.py:240
  1032.0 1.8 convert_element_type.293
  1033.8 1.8 convert_element_type.295
  1035.6 1.5 convert_element_type.296
  1037.1 1.5 convert_element_type.297
  1038.6 631.6 %reduce-scatter.2.cloned.1.call-done = bf16[2,128,32]{1,2,0:T(8,128)(2,1)} async-done(((bf16[64,128,32]{1,2,0:T(8,128)(2,1)}), bf16[2,128,32]{1,2,0:T(8,128)(2,1)}) %reduce-scatter.2.cloned.1.call-update) | async-done | bytes 16400 | tf_op jit(solution)/shard_map/reduce_scatter | solution.py:217
  1672.2 145.0 %psum.35 = bf16[256,64]{0,1:T(8,128)(2,1)S(1)} all-reduce(bf16[256,64]{0,1:T(8,128)(2,1)S(1)} %fusion.21), channel_id=1, replica_groups=mesh['crop'=16,'res'=32] {'res'}, use_global_device_ids=true, to_apply=%region_21.0 | all-reduce | flops 16384 | bytes 65536 | tf_op jit(solution)/shard_map/psum | solution.py:239
  (180 shorter events, 49.9 us)
Async XLA Ops:
  7.2 91.5 %copy-start = (bf16[1024,128]{1,0:T(8,128)(2,1)S(1)}, bf16[1024,128]{1,0:T(8,128)(2,1)}, u32[]{:S(2)}) copy-start(bf16[1024,128]{1,0:T(8,128)(2,1)} %param.12) | copy-start | bytes 786436
  7.2 230.1 %all-gather.5.cloned.1.call-start = ((), (), s32[]{:S(2)}) async-start(), calls=%async_computation.7 | async-start | bytes 1081344 | tf_op jit(solution)/shard_map/all_gather | solution.py:132
  8.3 1.1 copy-start.34
  8.3 90.3 %copy-start.29 = (bf16[2,64,128]{2,1,0:T(8,128)(2,1)S(1)}, bf16[2,64,128]{2,1,0:T(8,128)(2,1)}, u32[]{:S(2)}) copy-start(bf16[2,64,128]{2,1,0:T(8,128)(2,1)} %param.9) | copy-start | bytes 98308
  9.4 0.5 copy-start.36
  11.1 85.4 %copy-start.22 = (bf16[128,2,64]{0,2,1:T(8,128)(2,1)}, bf16[128,2,64]{0,2,1:T(8,128)(2,1)S(1)}, u32[]{:S(2)}) copy-start(bf16[128,2,64]{0,2,1:T(8,128)(2,1)S(1)} %convolution_convert_fusion) | copy-start | bytes 98308
  96.6 2.7 copy-start.14
  99.0 146.3 %copy-start.4 = (f32[2,64,128]{2,1,0:T(8,128)}, f32[2,64,128]{2,1,0:T(8,128)S(1)}, u32[]{:S(2)}) copy-start(f32[2,64,128]{2,1,0:T(8,128)S(1)} %get-tuple-element.84) | copy-start | bytes 196612
  99.5 0.7 copy-start.1
  100.9 277.3 %all-gather.11.cloned.1.call-start = ((), (), s32[]{:S(2)}) async-start(), calls=%async_computation.10 | async-start | bytes 1081344 | tf_op jit(solution)/shard_map/all_gather | solution.py:193
  101.6 417.4 %all-gather.7.cloned.1.call-start = ((), (), s32[]{:S(2)}) async-start(), calls=%async_computation.8 | async-start | bytes 1081344 | tf_op jit(solution)/shard_map/all_gather | solution.py:141
  244.3 138.6 %copy-start.31 = (f32[2,64]{1,0:T(2,128)}, f32[2,64]{1,0:T(2,128)S(1)}, u32[]{:S(2)}) copy-start(f32[2,64]{1,0:T(2,128)S(1)} %add_rsqrt_fusion.2) | copy-start | bytes 1540
  245.3 1.7 copy-start.16
  269.2 0.6 copy-start.10
  275.7 1.0 copy-start.12
  276.7 2.5 copy-start.21
  277.8 0.7 copy-start.3
  279.2 380.1 %all-gather.9.cloned.1.call-start = ((), (), s32[]{:S(2)}) async-start(), calls=%async_computation.9 | async-start | bytes 1081344 | tf_op jit(solution)/shard_map/all_gather | solution.py:165
  528.5 4.3 copy-start.33
  531.2 0.6 copy-start.17
  536.5 129.2 %all-to-all-start.3 = ((bf16[64,2,128]{2,1,0:T(2,128)(2,1)}), bf16[64,2,128]{2,1,0:T(2,128)(2,1)}, u32[]{:S(2)}, u32[]{:S(2)}) async-start(bf16[64,2,128]{2,1,0:T(2,128)(2,1)} %copy.215), calls=%async_computation.3 | async-start | bytes 65536 | tf_op jit(solution)/shard_map/all_to_all | solution.py:158
  667.2 34.2 %copy-start.32 = (f32[2,64]{1,0:T(2,128)S(1)}, f32[2,64]{1,0:T(2,128)}, u32[]{:S(2)}) copy-start(f32[2,64]{1,0:T(2,128)} %copy-done.31) | copy-start | bytes 1540
  670.1 36.2 %copy-start.5 = (f32[2,64,128]{2,1,0:T(8,128)S(1)}, f32[2,64,128]{2,1,0:T(8,128)}, u32[]{:S(2)}) copy-start(f32[2,64,128]{2,1,0:T(8,128)} %copy-done.4) | copy-start | bytes 196612
  672.7 1.2 copy-start.25
  672.7 1.2 copy-start.26
  672.7 3.3 copy-start.27
  672.7 3.3 copy-start.28
  676.7 22.4 %all-to-all-start.4 = ((bf16[64,2,128]{2,1,0:T(2,128)(2,1)}), bf16[64,2,128]{2,1,0:T(2,128)(2,1)}, u32[]{:S(2)}, u32[]{:S(2)}) async-start(bf16[64,2,128]{2,1,0:T(2,128)(2,1)} %copy.225), calls=%async_computation.4 | async-start | bytes 65536 | tf_op jit(solution)/shard_map/all_to_all | solution.py:177
  699.9 3.6 copy-start.7
  703.5 0.6 copy-start.11
  704.1 9.9 copy-start.19
  707.9 18.7 %all-to-all-start.5 = ((bf16[2,64,128]{2,0,1:T(2,128)(2,1)}), bf16[2,64,128]{2,0,1:T(2,128)(2,1)S(1)}, u32[]{:S(2)}, u32[]{:S(2)}) async-start(bf16[2,64,128]{2,0,1:T(2,128)(2,1)} %copy.230), calls=%async_computation.5 | async-start | bytes 65536 | tf_op jit(solution)/shard_map/all_to_all | solution.py:186
  711.8 320.2 %all-reduce.3.cloned.1.call-start = ((), (), s32[]{:S(2)}) async-start(), calls=%async_computation.12 | async-start | bytes 1310720 | tf_op jit(solution)/shard_map/psum | solution.py:240
  711.8 2.1 copy-start.20
  714.0 15.2 copy-start.2
  714.0 15.6 copy-start.15
  715.6 14.2 copy-start.13
  715.6 14.2 copy-start.24
  726.8 3.3 copy-start.8
  726.8 4.4 copy-start.18
  730.2 3.9 copy-start.9
  731.2 2.9 copy-start.23
  732.0 938.1 %reduce-scatter.2.cloned.1.call-start = ((), (), s32[]{:S(2)}) async-start(), calls=%async_computation.11 | async-start | bytes 540672 | tf_op jit(solution)/shard_map/reduce_scatter | solution.py:217
  732.3 3.2 copy-start.30
  757.4 912.8 %copy-start.6 = (bf16[128,2,256]{2,1,0:T(2,128)(2,1)S(1)}, bf16[128,2,256]{2,1,0:T(2,128)(2,1)}, u32[]{:S(2)}) copy-start(bf16[128,2,256]{2,1,0:T(2,128)(2,1)} %param.8) | copy-start | bytes 393220
  757.4 912.8 %copy-start.35 = (f32[128,2]{0,1:T(2,128)S(1)}, f32[128,2]{0,1:T(2,128)}, u32[]{:S(2)}) copy-start(f32[128,2]{0,1:T(2,128)} %copy-done.34) | copy-start | bytes 3076
  757.4 912.8 %copy-start.37 = (f32[128,2]{0,1:T(2,128)S(1)}, f32[128,2]{0,1:T(2,128)}, u32[]{:S(2)}) copy-start(f32[128,2]{0,1:T(2,128)} %copy-done.36) | copy-start | bytes 3076
  757.4 913.7 %copy-start.38 = (bf16[256,64]{0,1:T(8,128)(2,1)S(1)}, bf16[256,64]{0,1:T(8,128)(2,1)}, u32[]{:S(2)}) copy-start(bf16[256,64]{0,1:T(8,128)(2,1)} %param.11) | copy-start | bytes 98308
Sparse Core Ops, SparseCore 0:
  101.0 136.2 all-gather.4
  240.9 137.1 all-gather.10
  381.8 137.1 all-gather.6
  522.0 137.2 all-gather.8
  732.1 299.8 all-reduce.2
  1036.8 633.2 reduce-scatter.1
where the time goes:
time: 1830 us
  waiting for transfers between devices  1380 us (75%)
  blocking collectives  290 us (16%)
  local copies, waits for them, and re-layouts  52.4 us (3%)
  matrix products  41.7 us (2%)
  other arithmetic  23.2 us (1%)
  starting transfers between devices  19.2 us (1%)
    reduce_scatter x1, waiting for transfers between devices, on_device(): lax.psum_scatter(jnp.einsum('ijab,sia->jsb', block, outer_left, preferred...  632 us
    psum x1, waiting for transfers between devices, on_device(): lax.psum(mean_gradient.astype(jnp.bfloat16), 'res').astype(jnp.float32)  274 us
    psum x1, blocking collectives, on_device(): lax.psum(outer_gradient.astype(jnp.bfloat16), 'res').astype(jnp.float32)  145 us
    all_gather x1, waiting for transfers between devices, on_device(): first_right_all = lax.all_gather(first_right, 'res', axis=0, tiled=True)  135 us
    all_gather x1, waiting for transfers between devices, on_device(): left_all = lax.all_gather(column_left, 'res', axis=1, tiled=True)  132 us
    all_gather x1, waiting for transfers between devices, on_device(): lax.all_gather(column_right, 'res', axis=1, tiled=True)  111 us
    all_gather x1, blocking collectives, on_device(): outer_right = lax.all_gather(right_local, 'res', axis=1, tiled=True)  85.4 us
    all_gather x1, waiting for transfers between devices, on_device(): lax.all_gather(first_left, 'res', axis=0, tiled=True)  79.6 us
  transfers between devices with their start and end apart: 9, of which 8 were waited for; matrix products, arithmetic and copies ran while one was open for 4% of the time, Pallas kernels for 0%

commit v1 on v0

v1 whole, which is shorter than its diff:
```python
import functools

import jax
import jax.numpy as jnp
from jax import lax
from jax.experimental import pallas as pl
from jax.experimental.pallas import tpu as pltpu
from jax.sharding import PartitionSpec as P

EPS = 1e-05
F32 = jnp.float32
BF16 = jnp.bfloat16
MESH = pl.DeviceIdType.MESH

DEVICES = 32
ROWS = 2
RES = DEVICES * ROWS
CELLS = ROWS * RES
CH = 128
OUT = 32
SEQ = 128
MSA = 256
PER = CH // DEVICES
EARLY = 1024
LATE = 2048

NN = (((1,), (0,)), ((), ()))
NT = (((1,), (1,)), ((), ()))
TN = (((0,), (0,)), ((), ()))


def mul(a, b, dims=NN):
    return lax.dot_general(a, b, dims, preferred_element_type=F32)


def normalize(values, axis):
    shifted = values - jnp.mean(values, axis=axis, keepdims=True)
    inverse = lax.rsqrt(jnp.mean(shifted * shifted, axis=axis, keepdims=True) + EPS)
    return shifted * inverse, inverse


def norm_back(normed, inverse, upstream, axis):
    mean_upstream = jnp.mean(upstream, axis=axis, keepdims=True)
    mean_product = jnp.mean(upstream * normed, axis=axis, keepdims=True)
    return inverse * (upstream - mean_upstream - normed * mean_product)


def kernel(
    alignment_ref, pair_ref, cotangent_ref, outer_ref, mean_ref, mean_swapped_ref, triangle_ref, gating_ref, mixing_ref,
    updated_ref, alignment_grad_ref, pair_grad_ref, outer_grad_ref, mean_grad_ref, triangle_grad_ref, gating_grad_ref,
    mixing_grad_ref,
    left_own, right_own, left_all, right_all, aligned, aligned_inv, spread, outer_mean, pack,
    factor_send, factor_recv, mixed_send, mixed_recv, back_send, back_recv, grad_send, grad_recv, cot_send, cot_recv,
    left_chan, right_chan, triangle_t, normed_s, parts_s, gate_s, tail_s, logit_s, upstream_s,
    early_send, early_recv, early_own, early_all, late_send, late_recv, late_own, late_all,
    send_sem, recv_sem,
):
    me = lax.axis_index("res")
    other = lax.rem(me + 1, DEVICES)

    def each_peer(body):
        def step(k, carry):
            body(lax.rem(me + k, DEVICES))
            return carry

        lax.fori_loop(1, DEVICES, step, 0)

    def remote(source, target, phase, peer):
        return pltpu.make_async_remote_copy(
            src_ref=source, dst_ref=target, send_sem=send_sem.at[phase], recv_sem=recv_sem.at[phase],
            device_id={"res": peer}, device_id_type=MESH,
        )

    def exchange(send, recv, phase):
        each_peer(lambda peer: remote(send.at[peer], recv.at[me], phase, peer).start())
        recv[me] = send[me]

    def arrived(recv, phase):
        view = recv.at[pl.ds(0, DEVICES - 1)]
        remote(view, view, phase, other).wait_recv()

    def sent(send, phase):
        view = send.at[pl.ds(0, DEVICES - 1)]
        remote(view, view, phase, other).wait_send()

    barrier = pltpu.get_barrier_semaphore()
    each_peer(lambda peer: pl.semaphore_signal(barrier, inc=1, device_id={"res": peer}, device_id_type=MESH))

    for j in range(ROWS):
        normed, inverse = normalize(alignment_ref[j].astype(F32), 1)
        aligned[j] = normed
        aligned_inv[j] = inverse
        projected = mul(outer_ref[...], normed.astype(BF16), (((0,), (1,)), ((), ()))).astype(BF16)
        left_own[j] = projected[:OUT]
        right_own[j] = projected[OUT:]
    pl.semaphore_wait(barrier, DEVICES - 1)

    each_peer(lambda peer: remote(right_own, right_all.at[:, me], 0, peer).start())
    right_all[:, me] = right_own[...]
    each_peer(lambda peer: remote(left_own, left_all.at[:, me], 1, peer).start())
    left_all[:, me] = left_own[...]

    row = lax.broadcasted_iota(jnp.int32, (CELLS, CELLS), 0)
    column = lax.broadcasted_iota(jnp.int32, (CELLS, CELLS), 1)
    place = (row // RES) * RES + lax.rem(row, 2) * DEVICES + lax.rem(row, RES) // 2
    order = jnp.where(place == column, 1.0, 0.0).astype(BF16)
    pair = mul(pair_ref[...], order, TN)
    upstream_s[0] = mul(cotangent_ref[...], order, TN)
    for t in range(2):
        triangle_t[t, : 4 * CH] = triangle_ref[t].T
        triangle_t[t, 4 * CH : 5 * CH] = gating_ref[t].T
        triangle_t[t, 5 * CH :] = mixing_ref[t].T
    pack[...] = jnp.zeros_like(pack)
    early_send[...] = jnp.zeros_like(early_send)
    late_send[...] = jnp.zeros_like(late_send)

    def put(values, slot):
        for k in range(PER):
            pack[pl.ds(slot + k, DEVICES, stride=8), :] = values[k * DEVICES : (k + 1) * DEVICES]

    def post(send):
        send[...] = pack[...].reshape(DEVICES, 8, CELLS).astype(BF16)

    def take(recv):
        pack[...] = recv[...].astype(F32).reshape(DEVICES * 8, CELLS)

    def get(slot):
        return jnp.concatenate([pack[pl.ds(slot + k, DEVICES, stride=8), :] for k in range(PER)], axis=0)

    def channel(slot):
        values = pack[pl.ds(slot, DEVICES, stride=8), :]
        return jnp.concatenate([values[:, :RES], values[:, RES:]], axis=0).astype(BF16)

    def put_channel(values, slot):
        pack[pl.ds(slot, DEVICES, stride=8), :] = jnp.concatenate([values[:DEVICES], values[DEVICES:]], axis=1)

    view = right_all.at[:, pl.ds(0, DEVICES - 1)]
    remote(view, view, 0, other).wait_recv()
    spread[...] = mul(
        right_all[...].reshape(RES * OUT, SEQ), left_own[...].reshape(ROWS * OUT, SEQ), NT
    ) * (1.0 / SEQ)
    for b in range(OUT):
        piece = spread[pl.ds(b, RES, stride=OUT), :].astype(BF16)
        for i in range(ROWS):
            outer_mean[i * RES : (i + 1) * RES, b * OUT : (b + 1) * OUT] = piece[:, i * OUT : (i + 1) * OUT]
    pair = pair + mul(outer_mean[...], mean_swapped_ref[...]).T

    pair = pair.astype(BF16).astype(F32)
    for t in range(2):
        normed, inverse = normalize(pair, 0)
        normed_s[t] = normed
        half = normed.astype(BF16)
        projected = mul(triangle_t[t, : 5 * CH], half)
        parts_s[t, 0] = projected[:CH]
        parts_s[t, 1] = jax.nn.sigmoid(projected[CH : 2 * CH])
        parts_s[t, 2] = projected[2 * CH : 3 * CH]
        parts_s[t, 3] = jax.nn.sigmoid(projected[3 * CH : 4 * CH])
        gate_s[t] = jax.nn.sigmoid(projected[4 * CH :])
        put(parts_s[t, 0] * parts_s[t, 1], 0)
        put(parts_s[t, 2] * parts_s[t, 3], PER)
        post(factor_send.at[t])
        exchange(factor_send.at[t], factor_recv.at[t], 2 + t)
        tail_s[t, 2, :1] = inverse
        arrived(factor_recv.at[t], 2 + t)
        take(factor_recv.at[t])
        mixed = []
        for k in range(PER):
            left, right = channel(k), channel(PER + k)
            left_chan[t, k] = left
            right_chan[t, k] = right
            mixed.append(mul(left, right, NT if t == 0 else TN))
        for k in range(PER):
            put_channel(mixed[k], k)
        post(mixed_send.at[t])
        exchange(mixed_send.at[t], mixed_recv.at[t], 4 + t)
        arrived(mixed_recv.at[t], 4 + t)
        take(mixed_recv.at[t])
        mixed_norm, mixed_inverse = normalize(get(0), 0)
        update = mul(triangle_t[t, 5 * CH :], mixed_norm.astype(BF16))
        tail_s[t, 0] = mixed_norm
        tail_s[t, 1] = update
        tail_s[t, 2, 8:9] = mixed_inverse
        pair = (pair + gate_s[t] * update).astype(BF16).astype(F32)
    updated_ref[...] = pair.T.astype(BF16)

    def rows_of(t):
        return (early_send, 0) if t == 1 else (late_send, 0)

    for t in (1, 0):
        upstream = upstream_s[1 - t]
        gate = gate_s[t]
        mixed_norm = tail_s[t, 0]
        update_grad = (upstream * gate).astype(BF16)
        logit_grad = (upstream * tail_s[t, 1] * gate * (1.0 - gate)).astype(BF16)
        logit_s[t] = logit_grad
        mixed_grad = norm_back(mixed_norm, tail_s[t, 2, 8:9], mul(mixing_ref[t], update_grad), 0)
        put(mixed_grad, 0)
        post(back_send.at[t])
        exchange(back_send.at[t], back_recv.at[t], 6 + t)
        mixing_grad = mul(mixed_norm.astype(BF16), update_grad, NT).astype(BF16)
        half = normed_s[t].astype(BF16)
        gating_grad = mul(half, logit_grad, NT).astype(BF16)
        if t == 1:
            early_send[4 * CH : 5 * CH] = gating_grad
            early_send[5 * CH : 6 * CH] = mixing_grad
        else:
            early_send[6 * CH : 7 * CH] = mixing_grad
            late_send[4 * CH : 5 * CH] = gating_grad
            each_peer(
                lambda peer: remote(
                    early_send.at[pl.ds(pl.multiple_of(peer * (EARLY // DEVICES), EARLY // DEVICES), EARLY // DEVICES)],
                    early_recv.at[me], 10, peer,
                ).start()
            )
            early_recv[me] = early_send[pl.ds(pl.multiple_of(me * (EARLY // DEVICES), EARLY // DEVICES), EARLY // DEVICES)]
        arrived(back_recv.at[t], 6 + t)
        take(back_recv.at[t])
        grads = [channel(k) for k in range(PER)]
        for k in range(PER):
            grad, left, right = grads[k], left_chan[t, k], right_chan[t, k]
            if t == 0:
                left_grad, right_grad = mul(grad, right), mul(grad, left, TN)
            else:
                left_grad, right_grad = mul(right, grad, NT), mul(left, grad)
            put_channel(left_grad, k)
            put_channel(right_grad, PER + k)
        post(grad_send.at[t])
        exchange(grad_send.at[t], grad_recv.at[t], 8 + t)
        if t == 0:
            arrived(early_recv, 10)
            total = jnp.sum(early_recv[...].astype(F32), axis=0).astype(BF16)
            early_own[...] = total
            each_peer(lambda peer: remote(early_own, early_all.at[me], 11, peer).start())
            early_all[me] = total
        arrived(grad_recv.at[t], 8 + t)
        take(grad_recv.at[t])
        left_grad, right_grad = get(0), get(PER)
        linear, switch = parts_s[t, 0], parts_s[t, 1]
        one = (left_grad * switch).astype(BF16)
        two = (left_grad * linear * switch * (1.0 - switch)).astype(BF16)
        linear, switch = parts_s[t, 2], parts_s[t, 3]
        three = (right_grad * switch).astype(BF16)
        four = (right_grad * linear * switch * (1.0 - switch)).astype(BF16)
        quarter = jnp.concatenate([one, two, three, four], axis=0)
        normed_grad = mul(triangle_ref[t], quarter) + mul(gating_ref[t], logit_s[t])
        upstream = upstream + norm_back(normed_s[t], tail_s[t, 2, :1], normed_grad, 0)
        if t == 1:
            upstream_s[1] = upstream
        target = early_send if t == 1 else late_send
        project_grad = mul(half, quarter, NT).astype(BF16)
        for q in range(4):
            target[q * CH : (q + 1) * CH] = project_grad[:, q * CH : (q + 1) * CH]

    cells = upstream.T
    pair_grad_ref[...] = cells
    for k in range(4):
        pack[pl.ds(k, DEVICES, stride=8), :] = cells[k * DEVICES : (k + 1) * DEVICES]
    post(cot_send)
    exchange(cot_send, cot_recv, 12)
    own_cot = cells.astype(BF16)
    late_send[5 * CH : 13 * CH] = mul(outer_mean[...], own_cot, TN).astype(BF16)

    def factor_grad(cot, weight, factors):
        wide = (mul(cot, weight, NT) * (1.0 / SEQ)).astype(BF16).astype(F32)
        for b in range(OUT):
            piece = wide[:, b * OUT : (b + 1) * OUT]
            spread[pl.ds(b, RES, stride=OUT), :] = jnp.concatenate([piece[:RES], piece[RES:]], axis=1)
        return mul(spread[...].astype(BF16), factors[...].reshape(RES * OUT, SEQ), TN).astype(BF16)

    left_grad = factor_grad(own_cot, mean_swapped_ref[...], right_all)
    arrived(cot_recv, 12)
    take(cot_recv)
    theirs = [pack[pl.ds(k, DEVICES, stride=8), :] for k in range(4)]
    cot = jnp.concatenate([theirs[0], theirs[2], theirs[1], theirs[3]], axis=0).astype(BF16)
    view = left_all.at[:, pl.ds(0, DEVICES - 1)]
    remote(view, view, 1, other).wait_recv()
    right_grad = factor_grad(cot, mean_ref[...], left_all)

    grads = [
        jnp.concatenate([left_grad[j * OUT : (j + 1) * OUT], right_grad[j * OUT : (j + 1) * OUT]], axis=0)
        for j in range(ROWS)
    ]
    outer_grad = sum(mul(grads[j], aligned[j].astype(BF16)) for j in range(ROWS)).astype(BF16)
    late_send[13 * CH : 13 * CH + 2 * OUT] = outer_grad[:, :CH]
    late_send[13 * CH + 2 * OUT : 14 * CH] = outer_grad[:, CH:]
    share = LATE // DEVICES
    each_peer(
        lambda peer: remote(
            late_send.at[pl.ds(pl.multiple_of(peer * share, share), share)], late_recv.at[me], 13, peer
        ).start()
    )
    late_recv[me] = late_send[pl.ds(pl.multiple_of(me * share, share), share)]
    for j in range(ROWS):
        back = mul(grads[j], outer_ref[...], (((0,), (1,)), ((), ())))
        alignment_grad_ref[j] = norm_back(aligned[j], aligned_inv[j], back, 1)

    arrived(late_recv, 13)
    total = jnp.sum(late_recv[...].astype(F32), axis=0).astype(BF16)
    late_own[...] = total
    each_peer(lambda peer: remote(late_own, late_all.at[me], 14, peer).start())
    late_all[me] = total

    arrived(early_all, 11)
    early = early_all[...].reshape(EARLY, CH)
    for q in range(4):
        triangle_grad_ref[1, :, q * CH : (q + 1) * CH] = early[q * CH : (q + 1) * CH].astype(F32)
    gating_grad_ref[1] = early[4 * CH : 5 * CH].astype(F32)
    mixing_grad_ref[1] = early[5 * CH : 6 * CH].astype(F32)
    mixing_grad_ref[0] = early[6 * CH : 7 * CH].astype(F32)

    for own, phase in ((right_all, 0), (left_all, 1)):
        view = own.at[:, pl.ds(0, DEVICES - 1)]
        remote(view, view, phase, other).wait_send()
    for t in range(2):
        sent(factor_recv.at[t], 2 + t)
        sent(mixed_recv.at[t], 4 + t)
        sent(back_recv.at[t], 6 + t)
        sent(grad_recv.at[t], 8 + t)
    sent(early_recv, 10)
    sent(early_all, 11)
    sent(cot_recv, 12)
    sent(late_recv, 13)

    arrived(late_all, 14)
    late = late_all[...].reshape(LATE, CH)
    for q in range(4):
        triangle_grad_ref[0, :, q * CH : (q + 1) * CH] = late[q * CH : (q + 1) * CH].astype(F32)
    gating_grad_ref[0] = late[4 * CH : 5 * CH].astype(F32)
    mean_grad_ref[...] = late[5 * CH : 13 * CH].astype(F32)
    outer_grad_ref[:, :CH] = late[13 * CH : 13 * CH + 2 * OUT].astype(F32)
    outer_grad_ref[:, CH:] = late[13 * CH + 2 * OUT : 14 * CH].astype(F32)
    sent(late_all, 14)


def on_device(
    alignment, pair_features, pair_cotangent, outer_weight, mean_weight, triangle_weight, gating_weight, mixing_weight
):
    swapped = mean_weight.reshape(OUT, OUT, CH).swapaxes(0, 1).reshape(OUT * OUT, CH)
    message = pltpu.VMEM((2, DEVICES, 8, CELLS), BF16)
    half_early, half_late = EARLY // DEVICES, LATE // DEVICES
    updated, alignment_grad, pair_grad, outer_grad, mean_grad, triangle_grad, gating_grad, mixing_grad = pl.pallas_call(
        kernel,
        out_shape=[
            jax.ShapeDtypeStruct((CELLS, CH), BF16),
            jax.ShapeDtypeStruct((ROWS, SEQ, MSA), F32),
            jax.ShapeDtypeStruct((CELLS, CH), F32),
            jax.ShapeDtypeStruct((2 * OUT, MSA), F32),
            jax.ShapeDtypeStruct((OUT * OUT, CH), F32),
            jax.ShapeDtypeStruct((2, CH, 4 * CH), F32),
            jax.ShapeDtypeStruct((2, CH, CH), F32),
            jax.ShapeDtypeStruct((2, CH, CH), F32),
        ],
        in_specs=[pl.BlockSpec(memory_space=pltpu.VMEM)] * 9,
        out_specs=[pl.BlockSpec(memory_space=pltpu.VMEM)] * 8,
        scratch_shapes=[
            pltpu.VMEM((ROWS, OUT, SEQ), BF16),
            pltpu.VMEM((ROWS, OUT, SEQ), BF16),
            pltpu.VMEM((ROWS, DEVICES, OUT, SEQ), BF16),
            pltpu.VMEM((ROWS, DEVICES, OUT, SEQ), BF16),
            pltpu.VMEM((ROWS, SEQ, MSA), F32),
            pltpu.VMEM((ROWS, SEQ, 1), F32),
            pltpu.VMEM((RES * OUT, ROWS * OUT), F32),
            pltpu.VMEM((CELLS, OUT * OUT), BF16),
            pltpu.VMEM((DEVICES * 8, CELLS), F32),
            message, message, message, message, message, message, message, message,
            pltpu.VMEM((DEVICES, 8, CELLS), BF16),
            pltpu.VMEM((DEVICES, 8, CELLS), BF16),
            pltpu.VMEM((2, PER, RES, RES), BF16),
            pltpu.VMEM((2, PER, RES, RES), BF16),
            pltpu.VMEM((2, 6 * CH, CH), BF16),
            pltpu.VMEM((2, CH, CELLS), F32),
            pltpu.VMEM((2, 4, CH, CELLS), F32),
            pltpu.VMEM((2, CH, CELLS), F32),
            pltpu.VMEM((2, 3, CH, CELLS), F32),
            pltpu.VMEM((2, CH, CELLS), BF16),
            pltpu.VMEM((2, CH, CELLS), F32),
            pltpu.VMEM((EARLY, CH), BF16),
            pltpu.VMEM((DEVICES, half_early, CH), BF16),
            pltpu.VMEM((half_early, CH), BF16),
            pltpu.VMEM((DEVICES, half_early, CH), BF16),
            pltpu.VMEM((LATE, CH), BF16),
            pltpu.VMEM((DEVICES, half_late, CH), BF16),
            pltpu.VMEM((half_late, CH), BF16),
            pltpu.VMEM((DEVICES, half_late, CH), BF16),
            pltpu.SemaphoreType.DMA((15,)),
            pltpu.SemaphoreType.DMA((15,)),
        ],
        compiler_params=pltpu.CompilerParams(
            collective_id=0, has_side_effects=True, vmem_limit_bytes=40 * 1024 * 1024
        ),
        name="evoformer",
    )(
        alignment.swapaxes(0, 1),
        pair_features.reshape(CELLS, CH),
        pair_cotangent.reshape(CELLS, CH),
        outer_weight,
        mean_weight,
        swapped,
        triangle_weight,
        gating_weight,
        mixing_weight,
    )

    def natural(values):
        return values.reshape(ROWS, 2, DEVICES, CH).swapaxes(1, 2).reshape(ROWS, RES, CH)

    return (
        natural(updated),
        alignment_grad.swapaxes(0, 1),
        natural(pair_grad),
        outer_grad.T,
        mean_grad.reshape(OUT, OUT, CH).swapaxes(0, 1).reshape(OUT * OUT, CH),
        triangle_grad,
        gating_grad,
        mixing_grad,
    )


def solution(mesh):
    in_specs = (
        P("crop", "res", None),
        P("res", "crop", None),
        P("res", "crop", None),
        P(),
        P(),
        P(),
        P(),
        P(),
    )
    out_specs = (
        P("res", "crop", None),
        P("crop", "res", None),
        P("res", "crop", None),
        P("crop", None),
        P("crop", None),
        P("crop", None, None),
        P("crop", None, None),
        P("crop", None, None),
    )
    return jax.shard_map(
        on_device, mesh=mesh, in_specs=in_specs, out_specs=out_specs, check_vma=False
    )
```

time: 1830 us -> 212 us (0.12)
  waiting for transfers between devices: 1380 us -> 0 us
  blocking collectives: 290 us -> 0 us
  Pallas kernels: 0 us -> 199 us
  local copies, waits for them, and re-layouts: 52.4 us -> 8.82 us
  matrix products: 41.7 us -> 0 us
  other arithmetic: 23.2 us -> 0 us
  starting transfers between devices: 19.2 us -> 0 us
    reduce_scatter x1 -> x0, waiting for transfers between devices: 632 us -> none  [on_device(): lax.psum_scatter(jnp.einsum('ijab,sia->jsb', block, outer_left, preferred...]
    all_gather x4 -> x0, waiting for transfers between devices: 457 us -> none  [the longest x1 135 us: on_device(): first_right_all = lax.all_gather(first_right, 'res', axis=0, tiled=True)]
    psum x1 -> x0, waiting for transfers between devices: 274 us -> none  [on_device(): lax.psum(mean_gradient.astype(jnp.bfloat16), 'res').astype(jnp.float32)]
    pallas_call x0 -> x1, Pallas kernels: none -> 199 us  [on_device(): pl.pallas_call(kernel, out_shape=[jax.ShapeDtypeStruct((CELLS, CH), BF16)...]
    psum x1 -> x0, blocking collectives: 145 us -> none  [on_device(): lax.psum(outer_gradient.astype(jnp.bfloat16), 'res').astype(jnp.float32)]
    all_gather x1 -> x0, blocking collectives: 85.4 us -> none  [on_device(): outer_right = lax.all_gather(right_local, 'res', axis=1, tiled=True)]
    all_to_all x3 -> x0, blocking collectives: 59.7 us -> none  [the longest x1 22.2 us: on_device(): lax.all_to_all(second_pair, 'res', split_axis=1, concat_axis=0, tiled=True)]
    dot_general x33 -> x0, matrix products: 41.7 us -> none  [the longest x8 9.99 us: weight_gradient(): jnp.dot(flat_values.T, flat_upstream, preferred_element_type=jnp.float32)]
  transfers between devices with their start and end apart: 9 -> 0, of which waited for: 8 -> 0; matrix products, arithmetic and copies ran while one was open for 4% -> 0% of each run, Pallas kernels for 0% -> 0%
where the time goes in v1:
time: 212 us; the launch traced here: 209 us
  Pallas kernels  199 us (94%)
  local copies, waits for them, and re-layouts  8.82 us (4%)
    pallas_call x1, Pallas kernels, on_device(): pl.pallas_call(kernel, out_shape=[jax.ShapeDtypeStruct((CELLS, CH), BF16)...  199 us
    unnamed x19, local copies, waits for them, and re-layouts  6.29 us

profile of v1, /device:TPU:24, one launch (start us, length us, event | category | flops | bytes accessed | tf_op | source)
XLA Modules:
  0.0 208.5 jit_solution(15511597999845059861)
XLA Ops:
  0.6 0.0 copy-start
  0.6 0.9 copy.18.outer_ref
  1.6 0.9 copy.24
  2.5 0.0 copy-done
  2.5 0.0 copy-start.1
  2.5 0.0 copy-start.2
  2.5 0.0 copy-start.3
  2.5 0.0 copy-start.4
  2.5 0.0 copy-start.5
  2.6 0.1 copy.17
  2.7 0.8 copy-done.1
  3.5 0.0 copy-done.2
  3.5 0.0 copy-done.3
  3.5 0.0 copy-done.4
  3.5 0.0 copy-done.5
  3.5 199.0 %evoformer.1 = (bf16[128,128]{1,0:T(8,128)(2,1)S(1)}, f32[2,128,256]{2,1,0:T(8,128)S(1)}, f32[128,128]{1,0:T(8,128)S(1)}, f32[64,256]{1,0:T(8,128)S(1)}, f32[102...) custom-call(bf16[2,128,256]{2,1,0:T(8,128)(2,1)S(1)} %bitcast.25, ...), custom_call_target="tpu_custom_call" | custom-call | tf_op jit(solution)/shard_map/evoformer/pallas_call | solution.py:341
  202.5 0.6 copy.19
  203.1 0.9 copy.22
  204.0 0.7 copy.20
  204.7 1.1 copy.21
  205.8 0.6 copy.29
  206.4 0.8 copy.30
  207.2 0.7 copy.31
  207.9 0.7 copy.32
Async XLA Ops:
  0.6 1.9 copy-start
  2.5 1.0 copy-start.1
  2.5 0.9 copy-start.2
  2.5 0.9 copy-start.3
  2.5 0.9 copy-start.4
  2.5 0.9 copy-start.5

commit v2 on v1

--- a/solution.py
+++ b/solution.py
@@ -21,8 +21,12 @@
 SEQ = 128
 MSA = 256
 PER = CH // DEVICES
-EARLY = 1024
-LATE = 2048
+EARLY = 32
+LATE = 48
+CHIPS = 16
+FAR = ((2, 1), (2, 0), (1, 1), (3, 1), (1, 0), (3, 0), (0, 1))
+GRID = (4, 4, 2)
+
 
 NN = (((1,), (0,)), ((), ()))
 NT = (((1,), (1,)), ((), ()))
@@ -51,19 +55,26 @@
     mixing_grad_ref,
     left_own, right_own, left_all, right_all, aligned, aligned_inv, spread, outer_mean, pack,
     factor_send, factor_recv, mixed_send, mixed_recv, back_send, back_recv, grad_send, grad_recv, cot_send, cot_recv,
+    outer_send, outer_recv, outer_own, outer_all,
     left_chan, right_chan, triangle_t, normed_s, parts_s, gate_s, tail_s, logit_s, upstream_s,
-    early_send, early_recv, early_own, early_all, late_send, late_recv, late_own, late_all,
+    early_send, early_near, early_class, early_far, early_own, early_all,
+    late_send, late_near, late_class, late_far, late_own, late_all,
     send_sem, recv_sem,
 ):
     me = lax.axis_index("res")
     other = lax.rem(me + 1, DEVICES)
+    z, x = me // 2, lax.rem(me, 2)
+    group, kind = z // 4, lax.rem(z, 4)
 
     def each_peer(body):
+        body(lax.rem(me + DEVICES // 2, DEVICES))
+
         def step(k, carry):
-            body(lax.rem(me + k, DEVICES))
+            body(lax.rem(me + DEVICES // 2 + k, DEVICES))
+            body(lax.rem(me + DEVICES // 2 - k, DEVICES))
             return carry
 
-        lax.fori_loop(1, DEVICES, step, 0)
+        lax.fori_loop(1, DEVICES // 2, step, 0)
 
     def remote(source, target, phase, peer):
         return pltpu.make_async_remote_copy(
@@ -71,17 +82,84 @@
             device_id={"res": peer}, device_id_type=MESH,
         )
 
+    def received(view, phase):
+        remote(view, view, phase, other).wait_recv()
+
+    def left(view, phase):
+        remote(view, view, phase, other).wait_send()
+
     def exchange(send, recv, phase):
         each_peer(lambda peer: remote(send.at[peer], recv.at[me], phase, peer).start())
         recv[me] = send[me]
 
     def arrived(recv, phase):
-        view = recv.at[pl.ds(0, DEVICES - 1)]
-        remote(view, view, phase, other).wait_recv()
-
-    def sent(send, phase):
-        view = send.at[pl.ds(0, DEVICES - 1)]
-        remote(view, view, phase, other).wait_send()
+        received(recv.at[pl.ds(0, DEVICES - 1)], phase)
+
+    def sent(recv, phase):
+        left(recv.at[pl.ds(0, DEVICES - 1)], phase)
+
+    far_place = [(lax.rem(group + m, 4), 1 - x if flip else x) for m, flip in FAR]
+    far_peer = [(4 * g + kind) * 2 + xx for g, xx in far_place]
+    far_source = [(lax.rem(group + 4 - m, 4), 1 - x if flip else x) for m, flip in FAR]
+    near_kind = [lax.rem(kind + n, 4) for n in (1, 3, 2)]
+    near_peer = [lax.rem(z + step, CHIPS) * 2 + x for step in (1, CHIPS - 1, CHIPS + 2 - 4 * (kind // 2))]
+
+    def gather_far(own, whole, phase):
+        for k in range(len(FAR)):
+            remote(own, whole(group, kind, x), phase + k, far_peer[k]).start()
+
+    def gather_near(whole, phase):
+        for n in range(3):
+            remote(whole(slice(None), kind, slice(None)), whole(slice(None), kind, slice(None)), phase, near_peer[n]).start()
+
+    def forward_block(whole, g, xx, phase):
+        for n in range(3):
+            remote(whole(g, kind, xx), whole(g, kind, xx), phase, near_peer[n]).start()
+
+    def gather_forward(whole, far_phase, phase):
+        forward_block(whole, group, x, phase)
+        for k in reversed(range(len(FAR))):
+            g, xx = far_source[k]
+            received(whole(g, kind, xx), far_phase + k)
+            forward_block(whole, g, xx, phase)
+
+    def far_received(whole, phase):
+        for k, (g, xx) in enumerate(far_source):
+            received(whole(g, kind, xx), phase + k)
+
+    def gather_left(whole, far_phase, phase):
+        for k, (g, xx) in enumerate(far_source):
+            left(whole(g, kind, xx), far_phase + k)
+        left(whole(slice(None), pl.ds(0, 3), slice(None)), phase)
+
+    def near_received(whole, phase):
+        received(whole(slice(None), pl.ds(0, 3), slice(None)), phase)
+
+    def scatter_near(send, near, phase):
+        for n in range(3):
+            remote(send.at[:, near_kind[n]], near.at[n], phase, near_peer[n]).start()
+
+    def scatter_far(send, near, of_class, far, near_phase, phase):
+        received(near, near_phase)
+        of_class[...] = (send[:, kind].astype(F32) + jnp.sum(near[...].astype(F32), axis=0)).astype(BF16)
+        for k, (g, xx) in enumerate(far_place):
+            remote(of_class.at[g, xx], far.at[k + 1], phase, far_peer[k]).start()
+        far[0] = of_class[group, x]
+
+    def scatter_sum(far, own, whole, phase):
+        received(far.at[pl.ds(1, 7)], phase)
+        total = jnp.sum(far[...].astype(F32), axis=0).astype(BF16)
+        own[...] = total
+        whole[group, kind, x] = total
+
+    def scatter_left(near, far, near_phase, phase):
+        left(near, near_phase)
+        left(far.at[pl.ds(1, 7)], phase)
+
+    rights = lambda g, k, xx: right_all.at[:, g, k, xx]
+    lefts = lambda g, k, xx: left_all.at[:, g, k, xx]
+    earlies = lambda g, k, xx: early_all.at[g, k, xx]
+    lates = lambda g, k, xx: late_all.at[g, k, xx]
 
     barrier = pltpu.get_barrier_semaphore()
     each_peer(lambda peer: pl.semaphore_signal(barrier, inc=1, device_id={"res": peer}, device_id_type=MESH))
@@ -95,10 +173,9 @@
         right_own[j] = projected[OUT:]
     pl.semaphore_wait(barrier, DEVICES - 1)
 
-    each_peer(lambda peer: remote(right_own, right_all.at[:, me], 0, peer).start())
-    right_all[:, me] = right_own[...]
-    each_peer(lambda peer: remote(left_own, left_all.at[:, me], 1, peer).start())
-    left_all[:, me] = left_own[...]
+    gather_far(right_own, rights, 20)
+    right_all[:, group, kind, x] = right_own[...]
+    left_all[:, group, kind, x] = left_own[...]
 
     row = lax.broadcasted_iota(jnp.int32, (CELLS, CELLS), 0)
     column = lax.broadcasted_iota(jnp.int32, (CELLS, CELLS), 1)
@@ -111,8 +188,7 @@
         triangle_t[t, 4 * CH : 5 * CH] = gating_ref[t].T
         triangle_t[t, 5 * CH :] = mixing_ref[t].T
     pack[...] = jnp.zeros_like(pack)
-    early_send[...] = jnp.zeros_like(early_send)
-    late_send[...] = jnp.zeros_like(late_send)
+    gather_forward(rights, 20, 0)
 
     def put(values, slot):
         for k in range(PER):
@@ -134,8 +210,7 @@
     def put_channel(values, slot):
         pack[pl.ds(slot, DEVICES, stride=8), :] = jnp.concatenate([values[:DEVICES], values[DEVICES:]], axis=1)
 
-    view = right_all.at[:, pl.ds(0, DEVICES - 1)]
-    remote(view, view, 0, other).wait_recv()
+    near_received(rights, 0)
     spread[...] = mul(
         right_all[...].reshape(RES * OUT, SEQ), left_own[...].reshape(ROWS * OUT, SEQ), NT
     ) * (1.0 / SEQ)
@@ -161,18 +236,23 @@
         post(factor_send.at[t])
         exchange(factor_send.at[t], factor_recv.at[t], 2 + t)
         tail_s[t, 2, :1] = inverse
+        if t == 0:
+            gather_far(left_own, lefts, 27)
         arrived(factor_recv.at[t], 2 + t)
         take(factor_recv.at[t])
         mixed = []
         for k in range(PER):
-            left, right = channel(k), channel(PER + k)
-            left_chan[t, k] = left
-            right_chan[t, k] = right
-            mixed.append(mul(left, right, NT if t == 0 else TN))
+            left_k, right_k = channel(k), channel(PER + k)
+            left_chan[t, k] = left_k
+            right_chan[t, k] = right_k
+            mixed.append(mul(left_k, right_k, NT if t == 0 else TN))
         for k in range(PER):
             put_channel(mixed[k], k)
         post(mixed_send.at[t])
         exchange(mixed_send.at[t], mixed_recv.at[t], 4 + t)
+        if t == 0:
+            far_received(lefts, 27)
+            gather_near(lefts, 1)
         arrived(mixed_recv.at[t], 4 + t)
         take(mixed_recv.at[t])
         mixed_norm, mixed_inverse = normalize(get(0), 0)
@@ -183,9 +263,7 @@
         pair = (pair + gate_s[t] * update).astype(BF16).astype(F32)
     updated_ref[...] = pair.T.astype(BF16)
 
-    def rows_of(t):
-        return (early_send, 0) if t == 1 else (late_send, 0)
-
+    early = []
     for t in (1, 0):
         upstream = upstream_s[1 - t]
         gate = gate_s[t]
@@ -200,38 +278,25 @@
         mixing_grad = mul(mixed_norm.astype(BF16), update_grad, NT).astype(BF16)
         half = normed_s[t].astype(BF16)
         gating_grad = mul(half, logit_grad, NT).astype(BF16)
-        if t == 1:
-            early_send[4 * CH : 5 * CH] = gating_grad
-            early_send[5 * CH : 6 * CH] = mixing_grad
-        else:
-            early_send[6 * CH : 7 * CH] = mixing_grad
-            late_send[4 * CH : 5 * CH] = gating_grad
-            each_peer(
-                lambda peer: remote(
-                    early_send.at[pl.ds(pl.multiple_of(peer * (EARLY // DEVICES), EARLY // DEVICES), EARLY // DEVICES)],
-                    early_recv.at[me], 10, peer,
-                ).start()
-            )
-            early_recv[me] = early_send[pl.ds(pl.multiple_of(me * (EARLY // DEVICES), EARLY // DEVICES), EARLY // DEVICES)]
+        early += [gating_grad, mixing_grad]
+        if t == 0:
+            early_send[...] = jnp.concatenate(early, axis=0).reshape(GRID + (EARLY, CH))
+            scatter_near(early_send, early_near, 13)
         arrived(back_recv.at[t], 6 + t)
         take(back_recv.at[t])
         grads = [channel(k) for k in range(PER)]
         for k in range(PER):
-            grad, left, right = grads[k], left_chan[t, k], right_chan[t, k]
+            grad, left_k, right_k = grads[k], left_chan[t, k], right_chan[t, k]
             if t == 0:
-                left_grad, right_grad = mul(grad, right), mul(grad, left, TN)
+                left_grad, right_grad = mul(grad, right_k), mul(grad, left_k, TN)
             else:
-                left_grad, right_grad = mul(right, grad, NT), mul(left, grad)
+                left_grad, right_grad = mul(right_k, grad, NT), mul(left_k, grad)
             put_channel(left_grad, k)
             put_channel(right_grad, PER + k)
         post(grad_send.at[t])
         exchange(grad_send.at[t], grad_recv.at[t], 8 + t)
         if t == 0:
-            arrived(early_recv, 10)
-            total = jnp.sum(early_recv[...].astype(F32), axis=0).astype(BF16)
-            early_own[...] = total
-            each_peer(lambda peer: remote(early_own, early_all.at[me], 11, peer).start())
-            early_all[me] = total
+            scatter_far(early_send, early_near, early_class, early_far, 13, 14)
         arrived(grad_recv.at[t], 8 + t)
         take(grad_recv.at[t])
         left_grad, right_grad = get(0), get(PER)
@@ -246,19 +311,25 @@
         upstream = upstream + norm_back(normed_s[t], tail_s[t, 2, :1], normed_grad, 0)
         if t == 1:
             upstream_s[1] = upstream
-        target = early_send if t == 1 else late_send
         project_grad = mul(half, quarter, NT).astype(BF16)
-        for q in range(4):
-            target[q * CH : (q + 1) * CH] = project_grad[:, q * CH : (q + 1) * CH]
+        pieces = [project_grad[:, q * CH : (q + 1) * CH] for q in range(4)]
+        if t == 1:
+            early += pieces
+        else:
+            late = pieces
 
     cells = upstream.T
     pair_grad_ref[...] = cells
     for k in range(4):
         pack[pl.ds(k, DEVICES, stride=8), :] = cells[k * DEVICES : (k + 1) * DEVICES]
     post(cot_send)
-    exchange(cot_send, cot_recv, 12)
+    exchange(cot_send, cot_recv, 10)
     own_cot = cells.astype(BF16)
-    late_send[5 * CH : 13 * CH] = mul(outer_mean[...], own_cot, TN).astype(BF16)
+    late.append(mul(outer_mean[...], own_cot, TN).astype(BF16))
+    late_send[...] = jnp.concatenate(late, axis=0).reshape(GRID + (LATE, CH))
+    scatter_near(late_send, late_near, 16)
+    scatter_sum(early_far, early_own, early_all, 14)
+    gather_far(early_own, earlies, 34)
 
     def factor_grad(cot, weight, factors):
         wide = (mul(cot, weight, NT) * (1.0 / SEQ)).astype(BF16).astype(F32)
@@ -268,76 +339,83 @@
         return mul(spread[...].astype(BF16), factors[...].reshape(RES * OUT, SEQ), TN).astype(BF16)
 
     left_grad = factor_grad(own_cot, mean_swapped_ref[...], right_all)
-    arrived(cot_recv, 12)
+    scatter_far(late_send, late_near, late_class, late_far, 16, 17)
+    arrived(cot_recv, 10)
     take(cot_recv)
     theirs = [pack[pl.ds(k, DEVICES, stride=8), :] for k in range(4)]
     cot = jnp.concatenate([theirs[0], theirs[2], theirs[1], theirs[3]], axis=0).astype(BF16)
-    view = left_all.at[:, pl.ds(0, DEVICES - 1)]
-    remote(view, view, 1, other).wait_recv()
+    near_received(lefts, 1)
     right_grad = factor_grad(cot, mean_ref[...], left_all)
 
     grads = [
         jnp.concatenate([left_grad[j * OUT : (j + 1) * OUT], right_grad[j * OUT : (j + 1) * OUT]], axis=0)
         for j in range(ROWS)
     ]
-    outer_grad = sum(mul(grads[j], aligned[j].astype(BF16)) for j in range(ROWS)).astype(BF16)
-    late_send[13 * CH : 13 * CH + 2 * OUT] = outer_grad[:, :CH]
-    late_send[13 * CH + 2 * OUT : 14 * CH] = outer_grad[:, CH:]
-    share = LATE // DEVICES
-    each_peer(
-        lambda peer: remote(
-            late_send.at[pl.ds(pl.multiple_of(peer * share, share), share)], late_recv.at[me], 13, peer
-        ).start()
-    )
-    late_recv[me] = late_send[pl.ds(pl.multiple_of(me * share, share), share)]
+    outer_grad = sum(mul(grads[j], aligned[j].astype(BF16)) for j in range(ROWS))
+    put(jnp.concatenate([outer_grad[:, :CH], outer_grad[:, CH:]], axis=0), 0)
+    post(outer_send)
+    exchange(outer_send, outer_recv, 11)
+    far_received(earlies, 34)
+    gather_near(earlies, 15)
     for j in range(ROWS):
         back = mul(grads[j], outer_ref[...], (((0,), (1,)), ((), ())))
         alignment_grad_ref[j] = norm_back(aligned[j], aligned_inv[j], back, 1)
 
-    arrived(late_recv, 13)
-    total = jnp.sum(late_recv[...].astype(F32), axis=0).astype(BF16)
-    late_own[...] = total
-    each_peer(lambda peer: remote(late_own, late_all.at[me], 14, peer).start())
-    late_all[me] = total
-
-    arrived(early_all, 11)
-    early = early_all[...].reshape(EARLY, CH)
+    scatter_sum(late_far, late_own, late_all, 17)
+    gather_far(late_own, lates, 41)
+    arrived(outer_recv, 11)
+    total = jnp.sum(outer_recv[...].astype(F32), axis=0).astype(BF16)
+    outer_own[...] = total
+    each_peer(lambda peer: remote(outer_own, outer_all.at[me], 12, peer).start())
+    outer_all[me] = total
+    gather_forward(lates, 41, 18)
+
+    near_received(earlies, 15)
+    early = early_all[...].reshape(DEVICES * EARLY, CH)
+    gating_grad_ref[1] = early[:CH].astype(F32)
+    mixing_grad_ref[1] = early[CH : 2 * CH].astype(F32)
     for q in range(4):
-        triangle_grad_ref[1, :, q * CH : (q + 1) * CH] = early[q * CH : (q + 1) * CH].astype(F32)
-    gating_grad_ref[1] = early[4 * CH : 5 * CH].astype(F32)
-    mixing_grad_ref[1] = early[5 * CH : 6 * CH].astype(F32)
-    mixing_grad_ref[0] = early[6 * CH : 7 * CH].astype(F32)
-
-    for own, phase in ((right_all, 0), (left_all, 1)):
-        view = own.at[:, pl.ds(0, DEVICES - 1)]
-        remote(view, view, phase, other).wait_send()
+        triangle_grad_ref[1, :, q * CH : (q + 1) * CH] = early[(2 + q) * CH : (3 + q) * CH].astype(F32)
+    gating_grad_ref[0] = early[6 * CH : 7 * CH].astype(F32)
+    mixing_grad_ref[0] = early[7 * CH :].astype(F32)
+
+    gather_left(rights, 20, 0)
+    gather_left(lefts, 27, 1)
     for t in range(2):
         sent(factor_recv.at[t], 2 + t)
         sent(mixed_recv.at[t], 4 + t)
         sent(back_recv.at[t], 6 + t)
         sent(grad_recv.at[t], 8 + t)
-    sent(early_recv, 10)
-    sent(early_all, 11)
-    sent(cot_recv, 12)
-    sent(late_recv, 13)
-
-    arrived(late_all, 14)
-    late = late_all[...].reshape(LATE, CH)
+    sent(cot_recv, 10)
+    sent(outer_recv, 11)
+    sent(outer_all, 12)
+    scatter_left(early_near, early_far, 13, 14)
+    gather_left(earlies, 34, 15)
+    scatter_left(late_near, late_far, 16, 17)
+
+    arrived(outer_all, 12)
+    take(outer_all)
+    outer = get(0)
+    outer_grad_ref[:, :CH] = outer[: 2 * OUT]
+    outer_grad_ref[:, CH:] = outer[2 * OUT :]
+    near_received(lates, 18)
+    late = late_all[...].reshape(DEVICES * LATE, CH)
     for q in range(4):
         triangle_grad_ref[0, :, q * CH : (q + 1) * CH] = late[q * CH : (q + 1) * CH].astype(F32)
-    gating_grad_ref[0] = late[4 * CH : 5 * CH].astype(F32)
-    mean_grad_ref[...] = late[5 * CH : 13 * CH].astype(F32)
-    outer_grad_ref[:, :CH] = late[13 * CH : 13 * CH + 2 * OUT].astype(F32)
-    outer_grad_ref[:, CH:] = late[13 * CH + 2 * OUT : 14 * CH].astype(F32)
-    sent(late_all, 14)
+    mean_grad_ref[...] = late[4 * CH :].astype(F32)
+    gather_left(lates, 41, 18)
 
 
 def on_device(
     alignment, pair_features, pair_cotangent, outer_weight, mean_weight, triangle_weight, gating_weight, mixing_weight
 ):
     swapped = mean_weight.reshape(OUT, OUT, CH).swapaxes(0, 1).reshape(OUT * OUT, CH)
+
+    def sums(rows):
+        shapes = (GRID, (3, 4, 2), (4, 2), (8,), (), GRID)
+        return [pltpu.VMEM(shape + (rows, CH), BF16) for shape in shapes]
+
     message = pltpu.VMEM((2, DEVICES, 8, CELLS), BF16)
-    half_early, half_late = EARLY // DEVICES, LATE // DEVICES
     updated, alignment_grad, pair_grad, outer_grad, mean_grad, triangle_grad, gating_grad, mixing_grad = pl.pallas_call(
         kernel,
         out_shape=[
@@ -355,8 +433,8 @@
         scratch_shapes=[
             pltpu.VMEM((ROWS, OUT, SEQ), BF16),
             pltpu.VMEM((ROWS, OUT, SEQ), BF16),
-            pltpu.VMEM((ROWS, DEVICES, OUT, SEQ), BF16),
-            pltpu.VMEM((ROWS, DEVICES, OUT, SEQ), BF16),
+            pltpu.VMEM((ROWS,) + GRID + (OUT, SEQ), BF16),
+            pltpu.VMEM((ROWS,) + GRID + (OUT, SEQ), BF16),
             pltpu.VMEM((ROWS, SEQ, MSA), F32),
             pltpu.VMEM((ROWS, SEQ, 1), F32),
             pltpu.VMEM((RES * OUT, ROWS * OUT), F32),
@@ -364,6 +442,10 @@
             pltpu.VMEM((DEVICES * 8, CELLS), F32),
             message, message, message, message, message, message, message, message,
             pltpu.VMEM((DEVICES, 8, CELLS), BF16),
+            pltpu.VMEM((DEVICES, 8, CELLS), BF16),
+            pltpu.VMEM((DEVICES, 8, CELLS), BF16),
+            pltpu.VMEM((DEVICES, 8, CELLS), BF16),
+            pltpu.VMEM((8, CELLS), BF16),
             pltpu.VMEM((DEVICES, 8, CELLS), BF16),
             pltpu.VMEM((2, PER, RES, RES), BF16),
             pltpu.VMEM((2, PER, RES, RES), BF16),
@@ -374,16 +456,10 @@
             pltpu.VMEM((2, 3, CH, CELLS), F32),
             pltpu.VMEM((2, CH, CELLS), BF16),
             pltpu.VMEM((2, CH, CELLS), F32),
-            pltpu.VMEM((EARLY, CH), BF16),
-            pltpu.VMEM((DEVICES, half_early, CH), BF16),
-            pltpu.VMEM((half_early, CH), BF16),
-            pltpu.VMEM((DEVICES, half_early, CH), BF16),
-            pltpu.VMEM((LATE, CH), BF16),
-            pltpu.VMEM((DEVICES, half_late, CH), BF16),
-            pltpu.VMEM((half_late, CH), BF16),
-            pltpu.VMEM((DEVICES, half_late, CH), BF16),
-            pltpu.SemaphoreType.DMA((15,)),
-            pltpu.SemaphoreType.DMA((15,)),
+            *sums(EARLY),
+            *sums(LATE),
+            pltpu.SemaphoreType.DMA((48,)),
+            pltpu.SemaphoreType.DMA((48,)),
         ],
         compiler_params=pltpu.CompilerParams(
             collective_id=0, has_side_effects=True, vmem_limit_bytes=40 * 1024 * 1024

time: 212 us -> 154 us (0.73)
  Pallas kernels: 199 us -> 142 us
    pallas_call x1, Pallas kernels: 199 us -> 142 us  [on_device(): pl.pallas_call(kernel, out_shape=[jax.ShapeDtypeStruct((CELLS, CH), BF16)...]
where the time goes in v2:
time: 154 us; the launch traced here: 152 us
  Pallas kernels  142 us (92%)
  local copies, waits for them, and re-layouts  8.82 us (6%)
    pallas_call x1, Pallas kernels, on_device(): pl.pallas_call(kernel, out_shape=[jax.ShapeDtypeStruct((CELLS, CH), BF16)...  142 us
    unnamed x19, local copies, waits for them, and re-layouts  6.29 us

profile of v2, /device:TPU:24, one launch (start us, length us, event | category | flops | bytes accessed | tf_op | source)
XLA Modules:
  0.0 151.7 jit_solution(13355749157238990159)
XLA Ops:
  0.6 0.0 copy-start
  0.6 0.9 copy.18.outer_ref
  1.6 0.9 copy.24
  2.5 0.0 copy-done
  2.5 0.0 copy-start.1
  2.5 0.0 copy-start.2
  2.5 0.0 copy-start.3
  2.5 0.0 copy-start.4
  2.5 0.0 copy-start.5
  2.6 0.1 copy.17
  2.7 0.8 copy-done.1
  3.5 0.0 copy-done.2
  3.5 0.0 copy-done.3
  3.5 0.0 copy-done.4
  3.5 0.0 copy-done.5
  3.5 142.1 %evoformer.1 = (bf16[128,128]{1,0:T(8,128)(2,1)S(1)}, f32[2,128,256]{2,1,0:T(8,128)S(1)}, f32[128,128]{1,0:T(8,128)S(1)}, f32[64,256]{1,0:T(8,128)S(1)}, f32[102...) custom-call(bf16[2,128,256]{2,1,0:T(8,128)(2,1)S(1)} %bitcast.25, ...), custom_call_target="tpu_custom_call" | custom-call | tf_op jit(solution)/shard_map/evoformer/pallas_call | solution.py:419
  145.6 0.6 copy.19
  146.3 0.9 copy.22
  147.2 0.7 copy.20
  147.8 1.1 copy.21
  148.9 0.6 copy.29
  149.6 0.8 copy.30
  150.4 0.7 copy.31
  151.0 0.7 copy.32
Async XLA Ops:
  0.6 1.9 %copy-start = (bf16[1024,128]{1,0:T(8,128)(2,1)S(1)}, bf16[1024,128]{1,0:T(8,128)(2,1)}, u32[]{:S(2)}) copy-start(bf16[1024,128]{1,0:T(8,128)(2,1)} %mean_ref.1) | copy-start | bytes 786436
  2.5 1.0 copy-start.1
  2.5 0.9 copy-start.2
  2.5 0.9 copy-start.3
  2.5 0.9 copy-start.4
  2.5 0.9 copy-start.5

commit v3 on v2

--- a/solution.py
+++ b/solution.py
@@ -24,9 +24,9 @@
 EARLY = 32
 LATE = 48
 CHIPS = 16
-FAR = ((2, 1), (2, 0), (1, 1), (3, 1), (1, 0), (3, 0), (0, 1))
-GRID = (4, 4, 2)
-
+FAR = (2, 1, 3)
+NEAR = ((2, 1), (1, 1), (3, 1), (2, 0), (1, 0), (3, 0), (0, 1))
+GRID = (4, 8)
 
 NN = (((1,), (0,)), ((), ()))
 NT = (((1,), (1,)), ((), ()))
@@ -51,8 +51,7 @@
 
 def kernel(
     alignment_ref, pair_ref, cotangent_ref, outer_ref, mean_ref, mean_swapped_ref, triangle_ref, gating_ref, mixing_ref,
-    updated_ref, alignment_grad_ref, pair_grad_ref, outer_grad_ref, mean_grad_ref, triangle_grad_ref, gating_grad_ref,
-    mixing_grad_ref,
+    updated_ref, alignment_grad_ref, pair_grad_ref, outer_grad_ref, early_ref, late_ref,
     left_own, right_own, left_all, right_all, aligned, aligned_inv, spread, outer_mean, pack,
     factor_send, factor_recv, mixed_send, mixed_recv, back_send, back_recv, grad_send, grad_recv, cot_send, cot_recv,
     outer_send, outer_recv, outer_own, outer_all,
@@ -64,7 +63,7 @@
     me = lax.axis_index("res")
     other = lax.rem(me + 1, DEVICES)
     z, x = me // 2, lax.rem(me, 2)
-    group, kind = z // 4, lax.rem(z, 4)
+    group, kind, place = me // 8, lax.rem(z, 4), lax.rem(me, 8)
 
     def each_peer(body):
         body(lax.rem(me + DEVICES // 2, DEVICES))
@@ -98,68 +97,68 @@
     def sent(recv, phase):
         left(recv.at[pl.ds(0, DEVICES - 1)], phase)
 
-    far_place = [(lax.rem(group + m, 4), 1 - x if flip else x) for m, flip in FAR]
-    far_peer = [(4 * g + kind) * 2 + xx for g, xx in far_place]
-    far_source = [(lax.rem(group + 4 - m, 4), 1 - x if flip else x) for m, flip in FAR]
-    near_kind = [lax.rem(kind + n, 4) for n in (1, 3, 2)]
-    near_peer = [lax.rem(z + step, CHIPS) * 2 + x for step in (1, CHIPS - 1, CHIPS + 2 - 4 * (kind // 2))]
+    far_group = [lax.rem(group + m, 4) for m in FAR]
+    far_source = [lax.rem(group + 4 - m, 4) for m in FAR]
+    steps = {0: 0, 1: 1, 3: CHIPS - 1, 2: CHIPS + 2 - 4 * (kind // 2)}
+    near_x = [1 - x if flip else x for _, flip in NEAR]
+    near_place = [lax.rem(kind + step, 4) * 2 + xx for (step, _), xx in zip(NEAR, near_x)]
+    near_peer = [lax.rem(z + steps[step], CHIPS) * 2 + xx for (step, _), xx in zip(NEAR, near_x)]
 
     def gather_far(own, whole, phase):
-        for k in range(len(FAR)):
-            remote(own, whole(group, kind, x), phase + k, far_peer[k]).start()
+        for k, g in enumerate(far_group):
+            remote(own, whole(group, place), phase + k, 8 * g + place).start()
 
     def gather_near(whole, phase):
-        for n in range(3):
-            remote(whole(slice(None), kind, slice(None)), whole(slice(None), kind, slice(None)), phase, near_peer[n]).start()
-
-    def forward_block(whole, g, xx, phase):
-        for n in range(3):
-            remote(whole(g, kind, xx), whole(g, kind, xx), phase, near_peer[n]).start()
+        for peer in near_peer:
+            remote(whole(slice(None), place), whole(slice(None), place), phase, peer).start()
+
+    def forward_block(whole, g, phase):
+        for peer in near_peer:
+            remote(whole(g, place), whole(g, place), phase, peer).start()
 
     def gather_forward(whole, far_phase, phase):
-        forward_block(whole, group, x, phase)
+        forward_block(whole, group, phase)
         for k in reversed(range(len(FAR))):
-            g, xx = far_source[k]
-            received(whole(g, kind, xx), far_phase + k)
-            forward_block(whole, g, xx, phase)
+            received(whole(far_source[k], place), far_phase + k)
+            forward_block(whole, far_source[k], phase)
 
     def far_received(whole, phase):
-        for k, (g, xx) in enumerate(far_source):
-            received(whole(g, kind, xx), phase + k)
+        for k, g in enumerate(far_source):
+            received(whole(g, place), phase + k)
 
     def gather_left(whole, far_phase, phase):
-        for k, (g, xx) in enumerate(far_source):
-            left(whole(g, kind, xx), far_phase + k)
-        left(whole(slice(None), pl.ds(0, 3), slice(None)), phase)
+        for k, g in enumerate(far_source):
+            left(whole(g, place), far_phase + k)
+        left(whole(slice(None), pl.ds(0, 7)), phase)
 
     def near_received(whole, phase):
-        received(whole(slice(None), pl.ds(0, 3), slice(None)), phase)
+        received(whole(slice(None), pl.ds(0, 7)), phase)
 
     def scatter_near(send, near, phase):
-        for n in range(3):
-            remote(send.at[:, near_kind[n]], near.at[n], phase, near_peer[n]).start()
-
-    def scatter_far(send, near, of_class, far, near_phase, phase):
+        for n, peer in enumerate(near_peer):
+            remote(send.at[:, near_place[n]], near.at[n], phase, peer).start()
+
+    def scatter_far(send, near, of_place, far, near_phase, phase):
         received(near, near_phase)
-        of_class[...] = (send[:, kind].astype(F32) + jnp.sum(near[...].astype(F32), axis=0)).astype(BF16)
-        for k, (g, xx) in enumerate(far_place):
-            remote(of_class.at[g, xx], far.at[k + 1], phase, far_peer[k]).start()
-        far[0] = of_class[group, x]
+        of_place[...] = (send[:, place].astype(F32) + jnp.sum(near[...].astype(F32), axis=0)).astype(BF16)
+        for k, g in enumerate(far_group):
+            remote(of_place.at[g], far.at[k + 1], phase, 8 * g + place).start()
+        far[0] = of_place[group]
 
     def scatter_sum(far, own, whole, phase):
-        received(far.at[pl.ds(1, 7)], phase)
+        received(far.at[pl.ds(1, 3)], phase)
         total = jnp.sum(far[...].astype(F32), axis=0).astype(BF16)
         own[...] = total
-        whole[group, kind, x] = total
+        whole[group, place] = total
 
     def scatter_left(near, far, near_phase, phase):
         left(near, near_phase)
-        left(far.at[pl.ds(1, 7)], phase)
-
-    rights = lambda g, k, xx: right_all.at[:, g, k, xx]
-    lefts = lambda g, k, xx: left_all.at[:, g, k, xx]
-    earlies = lambda g, k, xx: early_all.at[g, k, xx]
-    lates = lambda g, k, xx: late_all.at[g, k, xx]
+        left(far.at[pl.ds(1, 3)], phase)
+
+    rights = lambda g, e: right_all.at[:, g, e]
+    lefts = lambda g, e: left_all.at[:, g, e]
+    earlies = lambda g, e: early_all.at[g, e]
+    lates = lambda g, e: late_all.at[g, e]
 
     barrier = pltpu.get_barrier_semaphore()
     each_peer(lambda peer: pl.semaphore_signal(barrier, inc=1, device_id={"res": peer}, device_id_type=MESH))
@@ -168,19 +167,19 @@
         normed, inverse = normalize(alignment_ref[j].astype(F32), 1)
         aligned[j] = normed
         aligned_inv[j] = inverse
-        projected = mul(outer_ref[...], normed.astype(BF16), (((0,), (1,)), ((), ()))).astype(BF16)
+        projected = mul(outer_ref[...], normed.astype(BF16), NT).astype(BF16)
         left_own[j] = projected[:OUT]
         right_own[j] = projected[OUT:]
     pl.semaphore_wait(barrier, DEVICES - 1)
 
     gather_far(right_own, rights, 20)
-    right_all[:, group, kind, x] = right_own[...]
-    left_all[:, group, kind, x] = left_own[...]
+    right_all[:, group, place] = right_own[...]
+    left_all[:, group, place] = left_own[...]
 
     row = lax.broadcasted_iota(jnp.int32, (CELLS, CELLS), 0)
     column = lax.broadcasted_iota(jnp.int32, (CELLS, CELLS), 1)
-    place = (row // RES) * RES + lax.rem(row, 2) * DEVICES + lax.rem(row, RES) // 2
-    order = jnp.where(place == column, 1.0, 0.0).astype(BF16)
+    kept = (row // RES) * RES + lax.rem(row, 2) * DEVICES + lax.rem(row, RES) // 2
+    order = jnp.where(kept == column, 1.0, 0.0).astype(BF16)
     pair = mul(pair_ref[...], order, TN)
     upstream_s[0] = mul(cotangent_ref[...], order, TN)
     for t in range(2):
@@ -261,7 +260,7 @@
         tail_s[t, 1] = update
         tail_s[t, 2, 8:9] = mixed_inverse
         pair = (pair + gate_s[t] * update).astype(BF16).astype(F32)
-    updated_ref[...] = pair.T.astype(BF16)
+    updated_ref[...] = mul(order, pair.astype(BF16), NT).astype(BF16)
 
     early = []
     for t in (1, 0):
@@ -282,6 +281,7 @@
         if t == 0:
             early_send[...] = jnp.concatenate(early, axis=0).reshape(GRID + (EARLY, CH))
             scatter_near(early_send, early_near, 13)
+            scatter_far(early_send, early_near, early_class, early_far, 13, 14)
         arrived(back_recv.at[t], 6 + t)
         take(back_recv.at[t])
         grads = [channel(k) for k in range(PER)]
@@ -296,7 +296,8 @@
         post(grad_send.at[t])
         exchange(grad_send.at[t], grad_recv.at[t], 8 + t)
         if t == 0:
-            scatter_far(early_send, early_near, early_class, early_far, 13, 14)
+            scatter_sum(early_far, early_own, early_all, 14)
+            gather_far(early_own, earlies, 34)
         arrived(grad_recv.at[t], 8 + t)
         take(grad_recv.at[t])
         left_grad, right_grad = get(0), get(PER)
@@ -319,7 +320,8 @@
             late = pieces
 
     cells = upstream.T
-    pair_grad_ref[...] = cells
+    for k in range(4):
+        pair_grad_ref[pl.ds((k // 2) * RES + k % 2, DEVICES, stride=2), :] = cells[k * DEVICES : (k + 1) * DEVICES]
     for k in range(4):
         pack[pl.ds(k, DEVICES, stride=8), :] = cells[k * DEVICES : (k + 1) * DEVICES]
     post(cot_send)
@@ -328,8 +330,6 @@
     late.append(mul(outer_mean[...], own_cot, TN).astype(BF16))
     late_send[...] = jnp.concatenate(late, axis=0).reshape(GRID + (LATE, CH))
     scatter_near(late_send, late_near, 16)
-    scatter_sum(early_far, early_own, early_all, 14)
-    gather_far(early_own, earlies, 34)
 
     def factor_grad(cot, weight, factors):
         wide = (mul(cot, weight, NT) * (1.0 / SEQ)).astype(BF16).astype(F32)
@@ -339,6 +339,8 @@
         return mul(spread[...].astype(BF16), factors[...].reshape(RES * OUT, SEQ), TN).astype(BF16)
 
     left_grad = factor_grad(own_cot, mean_swapped_ref[...], right_all)
+    far_received(earlies, 34)
+    gather_near(earlies, 15)
     scatter_far(late_send, late_near, late_class, late_far, 16, 17)
     arrived(cot_recv, 10)
     take(cot_recv)
@@ -355,10 +357,8 @@
     put(jnp.concatenate([outer_grad[:, :CH], outer_grad[:, CH:]], axis=0), 0)
     post(outer_send)
     exchange(outer_send, outer_recv, 11)
-    far_received(earlies, 34)
-    gather_near(earlies, 15)
     for j in range(ROWS):
-        back = mul(grads[j], outer_ref[...], (((0,), (1,)), ((), ())))
+        back = mul(grads[j], outer_ref[...], TN)
         alignment_grad_ref[j] = norm_back(aligned[j], aligned_inv[j], back, 1)
 
     scatter_sum(late_far, late_own, late_all, 17)
@@ -371,13 +371,7 @@
     gather_forward(lates, 41, 18)
 
     near_received(earlies, 15)
-    early = early_all[...].reshape(DEVICES * EARLY, CH)
-    gating_grad_ref[1] = early[:CH].astype(F32)
-    mixing_grad_ref[1] = early[CH : 2 * CH].astype(F32)
-    for q in range(4):
-        triangle_grad_ref[1, :, q * CH : (q + 1) * CH] = early[(2 + q) * CH : (3 + q) * CH].astype(F32)
-    gating_grad_ref[0] = early[6 * CH : 7 * CH].astype(F32)
-    mixing_grad_ref[0] = early[7 * CH :].astype(F32)
+    early_ref[...] = early_all[...].reshape(DEVICES * EARLY, CH)
 
     gather_left(rights, 20, 0)
     gather_left(lefts, 27, 1)
@@ -399,11 +393,29 @@
     outer_grad_ref[:, :CH] = outer[: 2 * OUT]
     outer_grad_ref[:, CH:] = outer[2 * OUT :]
     near_received(lates, 18)
-    late = late_all[...].reshape(DEVICES * LATE, CH)
+    late_ref[...] = late_all[...].reshape(DEVICES * LATE, CH)
+    gather_left(lates, 41, 18)
+
+
+def finish(
+    updated_ref, alignment_ref, pair_ref, outer_ref, early_ref, late_ref,
+    updated_out, alignment_out, pair_out, outer_out, mean_out, triangle_out, gating_out, mixing_out,
+):
+    updated_out[...] = updated_ref[...]
+    pair_out[...] = pair_ref[...]
+    outer_out[...] = outer_ref[...]
+    for j in range(ROWS):
+        alignment_out[:, j, :] = alignment_ref[j]
+
+    def early(k):
+        return early_ref[k * CH : (k + 1) * CH].astype(F32)
+
+    gating_out[1], mixing_out[1], gating_out[0], mixing_out[0] = early(0), early(1), early(6), early(7)
     for q in range(4):
-        triangle_grad_ref[0, :, q * CH : (q + 1) * CH] = late[q * CH : (q + 1) * CH].astype(F32)
-    mean_grad_ref[...] = late[4 * CH :].astype(F32)
-    gather_left(lates, 41, 18)
+        triangle_out[1, :, q * CH : (q + 1) * CH] = early(2 + q)
+        triangle_out[0, :, q * CH : (q + 1) * CH] = late_ref[q * CH : (q + 1) * CH].astype(F32)
+    for b in range(OUT):
+        mean_out[pl.ds(b, OUT, stride=OUT), :] = late_ref[4 * CH + b * OUT : 4 * CH + (b + 1) * OUT].astype(F32)
 
 
 def on_device(
@@ -412,24 +424,22 @@
     swapped = mean_weight.reshape(OUT, OUT, CH).swapaxes(0, 1).reshape(OUT * OUT, CH)
 
     def sums(rows):
-        shapes = (GRID, (3, 4, 2), (4, 2), (8,), (), GRID)
+        shapes = (GRID, (7, 4), (4,), (4,), (), GRID)
         return [pltpu.VMEM(shape + (rows, CH), BF16) for shape in shapes]
 
     message = pltpu.VMEM((2, DEVICES, 8, CELLS), BF16)
-    updated, alignment_grad, pair_grad, outer_grad, mean_grad, triangle_grad, gating_grad, mixing_grad = pl.pallas_call(
+    results = pl.pallas_call(
         kernel,
         out_shape=[
             jax.ShapeDtypeStruct((CELLS, CH), BF16),
             jax.ShapeDtypeStruct((ROWS, SEQ, MSA), F32),
             jax.ShapeDtypeStruct((CELLS, CH), F32),
             jax.ShapeDtypeStruct((2 * OUT, MSA), F32),
-            jax.ShapeDtypeStruct((OUT * OUT, CH), F32),
-            jax.ShapeDtypeStruct((2, CH, 4 * CH), F32),
-            jax.ShapeDtypeStruct((2, CH, CH), F32),
-            jax.ShapeDtypeStruct((2, CH, CH), F32),
+            jax.ShapeDtypeStruct((DEVICES * EARLY, CH), BF16),
+            jax.ShapeDtypeStruct((DEVICES * LATE, CH), BF16),
         ],
         in_specs=[pl.BlockSpec(memory_space=pltpu.VMEM)] * 9,
-        out_specs=[pl.BlockSpec(memory_space=pltpu.VMEM)] * 8,
+        out_specs=[pl.BlockSpec(memory_space=pltpu.VMEM)] * 6,
         scratch_shapes=[
             pltpu.VMEM((ROWS, OUT, SEQ), BF16),
             pltpu.VMEM((ROWS, OUT, SEQ), BF16),
@@ -469,7 +479,7 @@
         alignment.swapaxes(0, 1),
         pair_features.reshape(CELLS, CH),
         pair_cotangent.reshape(CELLS, CH),
-        outer_weight,
+        outer_weight.T,
         mean_weight,
         swapped,
         triangle_weight,
@@ -477,15 +487,29 @@
         mixing_weight,
     )
 
-    def natural(values):
-        return values.reshape(ROWS, 2, DEVICES, CH).swapaxes(1, 2).reshape(ROWS, RES, CH)
-
+    updated, alignment_grad, pair_grad, outer_grad, mean_grad, triangle_grad, gating_grad, mixing_grad = pl.pallas_call(
+        finish,
+        out_shape=[
+            jax.ShapeDtypeStruct((CELLS, CH), BF16),
+            jax.ShapeDtypeStruct((SEQ, ROWS, MSA), F32),
+            jax.ShapeDtypeStruct((CELLS, CH), F32),
+            jax.ShapeDtypeStruct((2 * OUT, MSA), F32),
+            jax.ShapeDtypeStruct((OUT * OUT, CH), F32),
+            jax.ShapeDtypeStruct((2, CH, 4 * CH), F32),
+            jax.ShapeDtypeStruct((2, CH, CH), F32),
+            jax.ShapeDtypeStruct((2, CH, CH), F32),
+        ],
+        in_specs=[pl.BlockSpec(memory_space=pltpu.VMEM)] * 6,
+        out_specs=[pl.BlockSpec(memory_space=pltpu.VMEM)] * 8,
+        compiler_params=pltpu.CompilerParams(vmem_limit_bytes=24 * 1024 * 1024),
+        name="finish",
+    )(*results)
     return (
-        natural(updated),
-        alignment_grad.swapaxes(0, 1),
-        natural(pair_grad),
+        updated.reshape(ROWS, RES, CH),
+        alignment_grad,
+        pair_grad.reshape(ROWS, RES, CH),
         outer_grad.T,
-        mean_grad.reshape(OUT, OUT, CH).swapaxes(0, 1).reshape(OUT * OUT, CH),
+        mean_grad,
         triangle_grad,
         gating_grad,
         mixing_grad,

time: 154 us -> 138 us (0.90); the launches traced: 152 us -> 138 us
  Pallas kernels: 142 us -> 135 us
  local copies, waits for them, and re-layouts: 8.82 us -> 1.93 us
    pallas_call x1, Pallas kernels: 142 us -> 134 us  [on_device(): pl.pallas_call(kernel, out_shape=[jax.ShapeDtypeStruct((CELLS, CH), BF16)...]
    unnamed x19 -> x15, local copies, waits for them, and re-layouts: 6.29 us -> 1.83 us
    transpose x3 -> x0, local copies, waits for them, and re-layouts: 2.42 us -> none  [the longest x2 1.32 us: natural(): values.reshape(ROWS, 2, DEVICES, CH).swapaxes(1, 2).reshape(ROWS, RES, CH)]
where the time goes in v3:
time: 138 us
  Pallas kernels  135 us (98%)
  local copies, waits for them, and re-layouts  1.93 us (1%)
    pallas_call x1, Pallas kernels, on_device(): pl.pallas_call(kernel, out_shape=[jax.ShapeDtypeStruct((CELLS, CH), BF16)...  134 us

profile of v3, /device:TPU:24, one launch (start us, length us, event | category | flops | bytes accessed | tf_op | source)
XLA Modules:
  0.0 138.1 jit_solution(14270851000096515990)
XLA Ops:
  0.6 0.0 copy-start
  0.6 1.0 copy.19
  1.6 0.0 copy-done
  1.6 0.0 copy-start.1
  1.6 0.0 copy-start.2
  1.7 0.0 copy-start.3
  1.7 0.0 copy-start.4
  1.7 0.0 copy-start.5
  1.7 0.0 copy-start.6
  1.7 0.1 copy.17
  1.8 0.8 copy-done.1
  2.6 0.0 copy-done.2
  2.6 0.0 copy-done.3
  2.6 0.0 copy-done.4
  2.6 0.0 copy-done.5
  2.6 0.0 copy-done.6
  2.6 134.0 %evoformer.1 = (bf16[128,128]{1,0:T(8,128)(2,1)S(1)}, f32[2,128,256]{2,1,0:T(8,128)S(1)}, f32[128,128]{1,0:T(8,128)S(1)}, f32[64,256]{1,0:T(8,128)S(1)}, bf16[10...) custom-call(bf16[2,128,256]{2,1,0:T(8,128)(2,1)S(1)} %bitcast.15, bf16[128,128]{1,0:T(8,128)(2,1)S(1)} %bitcast.16, ...), custom_call_target="tpu_custom_call" | custom-call | tf_op jit(solution)/shard_map/evoformer/pallas_call | solution.py:431
  136.7 1.5 %finish.1 = (bf16[128,128]{1,0:T(8,128)(2,1)}, f32[128,2,256]{2,1,0:T(2,128)}, f32[128,128]{1,0:T(8,128)}, f32[64,256]{1,0:T(8,128)}, f32[1024,128]{1,0:T(8,128)...) custom-call(bf16[128,128]{1,0:T(8,128)(2,1)S(1)} %get-tuple-element.22.updated_ref, ...), custom_call_target="tpu_custom_call" | custom-call | tf_op jit(solution)/shard_map/finish/pallas_call | solution.py:490
Async XLA Ops:
  0.6 1.0 copy-start
  1.6 0.9 copy-start.1
  1.6 1.0 copy-start.2
  1.7 1.0 copy-start.3
  1.7 1.0 copy-start.4
  1.7 0.9 copy-start.5
  1.7 0.9 copy-start.6

commit v4 on v3

--- a/solution.py
+++ b/solution.py
@@ -20,7 +20,7 @@
 OUT = 32
 SEQ = 128
 MSA = 256
-PER = CH // DEVICES
+PER = CH // 8
 EARLY = 32
 LATE = 48
 CHIPS = 16
@@ -53,9 +53,14 @@
     alignment_ref, pair_ref, cotangent_ref, outer_ref, mean_ref, mean_swapped_ref, triangle_ref, gating_ref, mixing_ref,
     updated_ref, alignment_grad_ref, pair_grad_ref, outer_grad_ref, early_ref, late_ref,
     left_own, right_own, left_all, right_all, aligned, aligned_inv, spread, outer_mean, pack,
-    factor_send, factor_recv, mixed_send, mixed_recv, back_send, back_recv, grad_send, grad_recv, cot_send, cot_recv,
-    outer_send, outer_recv, outer_own, outer_all,
-    left_chan, right_chan, triangle_t, normed_s, parts_s, gate_s, tail_s, logit_s, upstream_s,
+    wide_a, wide_b, wide_c,
+    left0_send, left0_recv, right0_send, right0_recv, mixed0_send, mixed0_recv,
+    factor1_send, factor1_recv, mixed1_send, mixed1_recv,
+    back1_send, back1_recv, grad1_send, grad1_recv,
+    back0_send, back0_recv, left_grad0_send, left_grad0_recv, right_grad0_send, right_grad0_recv,
+    cot_send, cot_recv,
+    outer_send, outer_near, outer_part, outer_far, outer_own, outer_all,
+    left0_chan, right0_chan, left1_chan, right1_chan, triangle_t, normed_s, parts_s, gate_s, tail_s, logit_s, upstream_s,
     early_send, early_near, early_class, early_far, early_own, early_all,
     late_send, late_near, late_class, late_far, late_own, late_all,
     send_sem, recv_sem,
@@ -91,6 +96,21 @@
         each_peer(lambda peer: remote(send.at[peer], recv.at[me], phase, peer).start())
         recv[me] = send[me]
 
+    def exchange_global(send, recv, phase):
+        each_peer(lambda peer: remote(send.at[lax.rem(peer, 8)], recv.at[me], phase, peer).start())
+        recv[me] = send[place]
+
+    def exchange_near(send, recv, phase):
+        for n, peer in enumerate(near_peer):
+            remote(send.at[near_place[n]], recv.at[place], phase, peer).start()
+        recv[place] = send[place]
+
+    def near_arrived(recv, phase):
+        received(recv.at[pl.ds(0, 7)], phase)
+
+    def near_sent(recv, phase):
+        left(recv.at[pl.ds(0, 7)], phase)
+
     def arrived(recv, phase):
         received(recv.at[pl.ds(0, DEVICES - 1)], phase)
 
@@ -116,11 +136,14 @@
         for peer in near_peer:
             remote(whole(g, place), whole(g, place), phase, peer).start()
 
+    def forward_arrived(whole, k, far_phase, phase):
+        received(whole(far_source[k], place), far_phase + k)
+        forward_block(whole, far_source[k], phase)
+
     def gather_forward(whole, far_phase, phase):
         forward_block(whole, group, phase)
         for k in reversed(range(len(FAR))):
-            received(whole(far_source[k], place), far_phase + k)
-            forward_block(whole, far_source[k], phase)
+            forward_arrived(whole, k, far_phase, phase)
 
     def far_received(whole, phase):
         for k, g in enumerate(far_source):
@@ -189,25 +212,34 @@
     pack[...] = jnp.zeros_like(pack)
     gather_forward(rights, 20, 0)
 
-    def put(values, slot):
-        for k in range(PER):
-            pack[pl.ds(slot + k, DEVICES, stride=8), :] = values[k * DEVICES : (k + 1) * DEVICES]
-
     def post(send):
         send[...] = pack[...].reshape(DEVICES, 8, CELLS).astype(BF16)
 
     def take(recv):
         pack[...] = recv[...].astype(F32).reshape(DEVICES * 8, CELLS)
 
-    def get(slot):
-        return jnp.concatenate([pack[pl.ds(slot + k, DEVICES, stride=8), :] for k in range(PER)], axis=0)
-
-    def channel(slot):
-        values = pack[pl.ds(slot, DEVICES, stride=8), :]
+    def shards(values):
+        return values.astype(BF16).reshape(8, PER, CELLS)
+
+    def whole(values):
+        return values.reshape(CH, CELLS).astype(F32)
+
+    def open_wide(wide, values, count):
+        wide[: count * PER] = values.astype(F32).reshape(count * PER, CELLS)
+
+    def channel(wide, k, count):
+        values = wide[pl.ds(k, count, stride=PER), :]
         return jnp.concatenate([values[:, :RES], values[:, RES:]], axis=0).astype(BF16)
 
-    def put_channel(values, slot):
-        pack[pl.ds(slot, DEVICES, stride=8), :] = jnp.concatenate([values[:DEVICES], values[DEVICES:]], axis=1)
+    def put_channel(wide, values, k, count):
+        wide[pl.ds(k, count, stride=PER), :] = jnp.concatenate([values[:count], values[count:]], axis=1)
+
+    def close_wide(wide, count):
+        return wide[: count * PER].reshape(count, PER, CELLS).astype(BF16)
+
+    def sum_groups(recv):
+        total = jnp.sum(recv[...].astype(F32).reshape(4, CH, CELLS), axis=0)
+        return total
 
     near_received(rights, 0)
     spread[...] = mul(
@@ -219,88 +251,86 @@
             outer_mean[i * RES : (i + 1) * RES, b * OUT : (b + 1) * OUT] = piece[:, i * OUT : (i + 1) * OUT]
     pair = pair + mul(outer_mean[...], mean_swapped_ref[...]).T
 
-    pair = pair.astype(BF16).astype(F32)
-    for t in range(2):
+    def head(t, pair):
         normed, inverse = normalize(pair, 0)
         normed_s[t] = normed
-        half = normed.astype(BF16)
-        projected = mul(triangle_t[t, : 5 * CH], half)
+        tail_s[t, 2, :1] = inverse
+        projected = mul(triangle_t[t, : 4 * CH], normed.astype(BF16))
         parts_s[t, 0] = projected[:CH]
         parts_s[t, 1] = jax.nn.sigmoid(projected[CH : 2 * CH])
         parts_s[t, 2] = projected[2 * CH : 3 * CH]
         parts_s[t, 3] = jax.nn.sigmoid(projected[3 * CH : 4 * CH])
-        gate_s[t] = jax.nn.sigmoid(projected[4 * CH :])
-        put(parts_s[t, 0] * parts_s[t, 1], 0)
-        put(parts_s[t, 2] * parts_s[t, 3], PER)
-        post(factor_send.at[t])
-        exchange(factor_send.at[t], factor_recv.at[t], 2 + t)
-        tail_s[t, 2, :1] = inverse
-        if t == 0:
-            gather_far(left_own, lefts, 27)
-        arrived(factor_recv.at[t], 2 + t)
-        take(factor_recv.at[t])
-        mixed = []
-        for k in range(PER):
-            left_k, right_k = channel(k), channel(PER + k)
-            left_chan[t, k] = left_k
-            right_chan[t, k] = right_k
-            mixed.append(mul(left_k, right_k, NT if t == 0 else TN))
-        for k in range(PER):
-            put_channel(mixed[k], k)
-        post(mixed_send.at[t])
-        exchange(mixed_send.at[t], mixed_recv.at[t], 4 + t)
-        if t == 0:
-            far_received(lefts, 27)
-            gather_near(lefts, 1)
-        arrived(mixed_recv.at[t], 4 + t)
-        take(mixed_recv.at[t])
-        mixed_norm, mixed_inverse = normalize(get(0), 0)
+        return shards(parts_s[t, 0] * parts_s[t, 1]), shards(parts_s[t, 2] * parts_s[t, 3])
+
+    def gate(t):
+        gate_s[t] = jax.nn.sigmoid(mul(triangle_t[t, 4 * CH : 5 * CH], normed_s[t].astype(BF16)))
+
+    def tail(t, pair, mixed):
+        mixed_norm, mixed_inverse = normalize(mixed, 0)
         update = mul(triangle_t[t, 5 * CH :], mixed_norm.astype(BF16))
         tail_s[t, 0] = mixed_norm
         tail_s[t, 1] = update
         tail_s[t, 2, 8:9] = mixed_inverse
-        pair = (pair + gate_s[t] * update).astype(BF16).astype(F32)
+        return (pair + gate_s[t] * update).astype(BF16).astype(F32)
+
+    pair = pair.astype(BF16).astype(F32)
+    left_factor, right_factor = head(0, pair)
+    right0_send[...] = right_factor
+    exchange_global(right0_send, right0_recv, 2)
+    left0_send[...] = left_factor
+    exchange_near(left0_send, left0_recv, 3)
+    gate(0)
+    near_arrived(left0_recv, 3)
+    open_wide(wide_a, left0_recv[...], 8)
+    for k in range(PER):
+        left0_chan[k] = channel(wide_a, k, 8)
+    arrived(right0_recv, 2)
+    open_wide(wide_b, right0_recv[...], DEVICES)
+    for k in range(PER):
+        right_k = channel(wide_b, k, DEVICES)
+        right0_chan[k] = right_k
+        put_channel(wide_c, mul(left0_chan[k], right_k, NT), k, 8)
+    mixed0_send[...] = close_wide(wide_c, 8)
+    exchange_near(mixed0_send, mixed0_recv, 4)
+    gather_far(left_own, lefts, 27)
+    near_arrived(mixed0_recv, 4)
+    pair = tail(0, pair, whole(mixed0_recv[...]))
+
+    left_factor, right_factor = head(1, pair)
+    factor1_send[:, 0] = left_factor
+    factor1_send[:, 1] = right_factor
+    exchange_near(factor1_send, factor1_recv, 5)
+    forward_block(lefts, group, 1)
+    gate(1)
+    near_arrived(factor1_recv, 5)
+    open_wide(wide_a, factor1_recv[:, 0], 8)
+    open_wide(wide_b, factor1_recv[:, 1], 8)
+    for k in range(PER):
+        left_k, right_k = channel(wide_a, k, 8), channel(wide_b, k, 8)
+        left1_chan[k] = left_k
+        right1_chan[k] = right_k
+        put_channel(wide_c, mul(left_k, right_k, TN), k, DEVICES)
+    mixed1_send[...] = close_wide(wide_c, DEVICES)
+    exchange(mixed1_send, mixed1_recv, 6)
+    arrived(mixed1_recv, 6)
+    pair = tail(1, pair, sum_groups(mixed1_recv))
     updated_ref[...] = mul(order, pair.astype(BF16), NT).astype(BF16)
 
-    early = []
-    for t in (1, 0):
-        upstream = upstream_s[1 - t]
-        gate = gate_s[t]
+    def tail_back(t, upstream):
+        gated = gate_s[t]
         mixed_norm = tail_s[t, 0]
-        update_grad = (upstream * gate).astype(BF16)
-        logit_grad = (upstream * tail_s[t, 1] * gate * (1.0 - gate)).astype(BF16)
+        update_grad = (upstream * gated).astype(BF16)
+        mixed_grad = norm_back(mixed_norm, tail_s[t, 2, 8:9], mul(mixing_ref[t], update_grad), 0)
+        return update_grad, shards(mixed_grad)
+
+    def tail_weights(t, upstream, update_grad):
+        gated = gate_s[t]
+        logit_grad = (upstream * tail_s[t, 1] * gated * (1.0 - gated)).astype(BF16)
         logit_s[t] = logit_grad
-        mixed_grad = norm_back(mixed_norm, tail_s[t, 2, 8:9], mul(mixing_ref[t], update_grad), 0)
-        put(mixed_grad, 0)
-        post(back_send.at[t])
-        exchange(back_send.at[t], back_recv.at[t], 6 + t)
-        mixing_grad = mul(mixed_norm.astype(BF16), update_grad, NT).astype(BF16)
-        half = normed_s[t].astype(BF16)
-        gating_grad = mul(half, logit_grad, NT).astype(BF16)
-        early += [gating_grad, mixing_grad]
-        if t == 0:
-            early_send[...] = jnp.concatenate(early, axis=0).reshape(GRID + (EARLY, CH))
-            scatter_near(early_send, early_near, 13)
-            scatter_far(early_send, early_near, early_class, early_far, 13, 14)
-        arrived(back_recv.at[t], 6 + t)
-        take(back_recv.at[t])
-        grads = [channel(k) for k in range(PER)]
-        for k in range(PER):
-            grad, left_k, right_k = grads[k], left_chan[t, k], right_chan[t, k]
-            if t == 0:
-                left_grad, right_grad = mul(grad, right_k), mul(grad, left_k, TN)
-            else:
-                left_grad, right_grad = mul(right_k, grad, NT), mul(left_k, grad)
-            put_channel(left_grad, k)
-            put_channel(right_grad, PER + k)
-        post(grad_send.at[t])
-        exchange(grad_send.at[t], grad_recv.at[t], 8 + t)
-        if t == 0:
-            scatter_sum(early_far, early_own, early_all, 14)
-            gather_far(early_own, earlies, 34)
-        arrived(grad_recv.at[t], 8 + t)
-        take(grad_recv.at[t])
-        left_grad, right_grad = get(0), get(PER)
+        mixing_grad = mul(tail_s[t, 0].astype(BF16), update_grad, NT).astype(BF16)
+        return [mul(normed_s[t].astype(BF16), logit_grad, NT).astype(BF16), mixing_grad]
+
+    def head_back(t, upstream, left_grad, right_grad):
         linear, switch = parts_s[t, 0], parts_s[t, 1]
         one = (left_grad * switch).astype(BF16)
         two = (left_grad * linear * switch * (1.0 - switch)).astype(BF16)
@@ -309,27 +339,67 @@
         four = (right_grad * linear * switch * (1.0 - switch)).astype(BF16)
         quarter = jnp.concatenate([one, two, three, four], axis=0)
         normed_grad = mul(triangle_ref[t], quarter) + mul(gating_ref[t], logit_s[t])
-        upstream = upstream + norm_back(normed_s[t], tail_s[t, 2, :1], normed_grad, 0)
-        if t == 1:
-            upstream_s[1] = upstream
-        project_grad = mul(half, quarter, NT).astype(BF16)
-        pieces = [project_grad[:, q * CH : (q + 1) * CH] for q in range(4)]
-        if t == 1:
-            early += pieces
-        else:
-            late = pieces
+        return quarter, upstream + norm_back(normed_s[t], tail_s[t, 2, :1], normed_grad, 0)
+
+    def head_weights(t, quarter):
+        project_grad = mul(normed_s[t].astype(BF16), quarter, NT).astype(BF16)
+        return [project_grad[:, q * CH : (q + 1) * CH] for q in range(4)]
+
+    upstream = upstream_s[0]
+    update_grad, back1_send[...] = tail_back(1, upstream)
+    exchange_global(back1_send, back1_recv, 7)
+    early = tail_weights(1, upstream, update_grad)
+    arrived(back1_recv, 7)
+    open_wide(wide_a, back1_recv[...], DEVICES)
+    for k in range(PER):
+        grad = channel(wide_a, k, DEVICES)
+        put_channel(wide_b, mul(right1_chan[k], grad, NT), k, 8)
+        put_channel(wide_c, mul(left1_chan[k], grad), k, 8)
+    grad1_send[:, 0] = close_wide(wide_b, 8)
+    grad1_send[:, 1] = close_wide(wide_c, 8)
+    exchange_near(grad1_send, grad1_recv, 8)
+    forward_arrived(lefts, 1, 27, 1)
+    forward_arrived(lefts, 2, 27, 1)
+    near_arrived(grad1_recv, 8)
+    quarter, upstream = head_back(1, upstream, whole(grad1_recv[:, 0]), whole(grad1_recv[:, 1]))
+
+    update_grad, back0_send[...] = tail_back(0, upstream)
+    exchange_near(back0_send, back0_recv, 9)
+    forward_arrived(lefts, 0, 27, 1)
+    early += head_weights(1, quarter)
+    early += tail_weights(0, upstream, update_grad)
+    early_send[...] = jnp.concatenate(early, axis=0).reshape(GRID + (EARLY, CH))
+    scatter_near(early_send, early_near, 13)
+    near_arrived(back0_recv, 9)
+    open_wide(wide_a, back0_recv[...], 8)
+    grads = []
+    for k in range(PER):
+        grads.append(channel(wide_a, k, 8))
+        put_channel(wide_b, mul(grads[k], left0_chan[k], TN), k, DEVICES)
+    right_grad0_send[...] = close_wide(wide_b, DEVICES)
+    exchange(right_grad0_send, right_grad0_recv, 45)
+    for k in range(PER):
+        put_channel(wide_c, mul(grads[k], right0_chan[k]), k, 8)
+    left_grad0_send[...] = close_wide(wide_c, 8)
+    exchange_near(left_grad0_send, left_grad0_recv, 44)
+    scatter_far(early_send, early_near, early_class, early_far, 13, 14)
+    near_arrived(left_grad0_recv, 44)
+    arrived(right_grad0_recv, 45)
+    quarter, upstream = head_back(0, upstream, whole(left_grad0_recv[...]), sum_groups(right_grad0_recv))
 
     cells = upstream.T
-    for k in range(4):
-        pair_grad_ref[pl.ds((k // 2) * RES + k % 2, DEVICES, stride=2), :] = cells[k * DEVICES : (k + 1) * DEVICES]
+    own_cot = cells.astype(BF16)
+    late = head_weights(0, quarter) + [mul(outer_mean[...], own_cot, TN).astype(BF16)]
+    late_send[...] = jnp.concatenate(late, axis=0).reshape(GRID + (LATE, CH))
+    scatter_near(late_send, late_near, 16)
     for k in range(4):
         pack[pl.ds(k, DEVICES, stride=8), :] = cells[k * DEVICES : (k + 1) * DEVICES]
     post(cot_send)
     exchange(cot_send, cot_recv, 10)
-    own_cot = cells.astype(BF16)
-    late.append(mul(outer_mean[...], own_cot, TN).astype(BF16))
-    late_send[...] = jnp.concatenate(late, axis=0).reshape(GRID + (LATE, CH))
-    scatter_near(late_send, late_near, 16)
+    for k in range(4):
+        pair_grad_ref[pl.ds((k // 2) * RES + k % 2, DEVICES, stride=2), :] = cells[k * DEVICES : (k + 1) * DEVICES]
+    scatter_sum(early_far, early_own, early_all, 14)
+    gather_far(early_own, earlies, 34)
 
     def factor_grad(cot, weight, factors):
         wide = (mul(cot, weight, NT) * (1.0 / SEQ)).astype(BF16).astype(F32)
@@ -339,8 +409,6 @@
         return mul(spread[...].astype(BF16), factors[...].reshape(RES * OUT, SEQ), TN).astype(BF16)
 
     left_grad = factor_grad(own_cot, mean_swapped_ref[...], right_all)
-    far_received(earlies, 34)
-    gather_near(earlies, 15)
     scatter_far(late_send, late_near, late_class, late_far, 16, 17)
     arrived(cot_recv, 10)
     take(cot_recv)
@@ -354,42 +422,56 @@
         for j in range(ROWS)
     ]
     outer_grad = sum(mul(grads[j], aligned[j].astype(BF16)) for j in range(ROWS))
-    put(jnp.concatenate([outer_grad[:, :CH], outer_grad[:, CH:]], axis=0), 0)
-    post(outer_send)
-    exchange(outer_send, outer_recv, 11)
+    outer_grad = jnp.concatenate([outer_grad[:, :CH], outer_grad[:, CH:]], axis=0)
+    outer_send[...] = outer_grad.astype(BF16).reshape(8, 16, CH)
+    exchange_near(outer_send, outer_near, 11)
     for j in range(ROWS):
         back = mul(grads[j], outer_ref[...], TN)
         alignment_grad_ref[j] = norm_back(aligned[j], aligned_inv[j], back, 1)
 
+    far_received(earlies, 34)
+    gather_near(earlies, 15)
     scatter_sum(late_far, late_own, late_all, 17)
     gather_far(late_own, lates, 41)
-    arrived(outer_recv, 11)
-    total = jnp.sum(outer_recv[...].astype(F32), axis=0).astype(BF16)
+    near_arrived(outer_near, 11)
+    total = jnp.sum(outer_near[...].astype(F32), axis=0).astype(BF16)
+    outer_part[...] = total
+    for g in far_group:
+        remote(outer_part, outer_far.at[group], 12, 8 * g + place).start()
+    outer_far[group] = total
+    gather_forward(lates, 41, 18)
+    received(outer_far.at[pl.ds(0, 3)], 12)
+    total = jnp.sum(outer_far[...].astype(F32), axis=0).astype(BF16)
     outer_own[...] = total
-    each_peer(lambda peer: remote(outer_own, outer_all.at[me], 12, peer).start())
-    outer_all[me] = total
-    gather_forward(lates, 41, 18)
+    for peer in near_peer:
+        remote(outer_own, outer_all.at[place], 46, peer).start()
+    outer_all[place] = total
 
     near_received(earlies, 15)
     early_ref[...] = early_all[...].reshape(DEVICES * EARLY, CH)
 
     gather_left(rights, 20, 0)
     gather_left(lefts, 27, 1)
-    for t in range(2):
-        sent(factor_recv.at[t], 2 + t)
-        sent(mixed_recv.at[t], 4 + t)
-        sent(back_recv.at[t], 6 + t)
-        sent(grad_recv.at[t], 8 + t)
+    sent(right0_recv, 2)
+    near_sent(left0_recv, 3)
+    near_sent(mixed0_recv, 4)
+    near_sent(factor1_recv, 5)
+    sent(mixed1_recv, 6)
+    sent(back1_recv, 7)
+    near_sent(grad1_recv, 8)
+    near_sent(back0_recv, 9)
+    near_sent(left_grad0_recv, 44)
+    sent(right_grad0_recv, 45)
     sent(cot_recv, 10)
-    sent(outer_recv, 11)
-    sent(outer_all, 12)
+    near_sent(outer_near, 11)
+    left(outer_far.at[pl.ds(0, 3)], 12)
+    near_sent(outer_all, 46)
     scatter_left(early_near, early_far, 13, 14)
     gather_left(earlies, 34, 15)
     scatter_left(late_near, late_far, 16, 17)
 
-    arrived(outer_all, 12)
-    take(outer_all)
-    outer = get(0)
+    near_arrived(outer_all, 46)
+    outer = outer_all[...].reshape(CH, CH).astype(F32)
     outer_grad_ref[:, :CH] = outer[: 2 * OUT]
     outer_grad_ref[:, CH:] = outer[2 * OUT :]
     near_received(lates, 18)
@@ -427,7 +509,9 @@
         shapes = (GRID, (7, 4), (4,), (4,), (), GRID)
         return [pltpu.VMEM(shape + (rows, CH), BF16) for shape in shapes]
 
-    message = pltpu.VMEM((2, DEVICES, 8, CELLS), BF16)
+    near = pltpu.VMEM((8, PER, CELLS), BF16)
+    near_two = pltpu.VMEM((8, 2, PER, CELLS), BF16)
+    all_ = pltpu.VMEM((DEVICES, PER, CELLS), BF16)
     results = pl.pallas_call(
         kernel,
         out_shape=[
@@ -450,15 +534,25 @@
             pltpu.VMEM((RES * OUT, ROWS * OUT), F32),
             pltpu.VMEM((CELLS, OUT * OUT), BF16),
             pltpu.VMEM((DEVICES * 8, CELLS), F32),
-            message, message, message, message, message, message, message, message,
+            pltpu.VMEM((DEVICES * PER, CELLS), F32),
+            pltpu.VMEM((DEVICES * PER, CELLS), F32),
+            pltpu.VMEM((DEVICES * PER, CELLS), F32),
+            near, near, near, all_, near, near,
+            near_two, near_two, all_, all_,
+            near, all_, near_two, near_two,
+            near, near, near, near, all_, all_,
             pltpu.VMEM((DEVICES, 8, CELLS), BF16),
             pltpu.VMEM((DEVICES, 8, CELLS), BF16),
-            pltpu.VMEM((DEVICES, 8, CELLS), BF16),
-            pltpu.VMEM((DEVICES, 8, CELLS), BF16),
-            pltpu.VMEM((8, CELLS), BF16),
-            pltpu.VMEM((DEVICES, 8, CELLS), BF16),
-            pltpu.VMEM((2, PER, RES, RES), BF16),
-            pltpu.VMEM((2, PER, RES, RES), BF16),
+            pltpu.VMEM((8, 16, CH), BF16),
+            pltpu.VMEM((8, 16, CH), BF16),
+            pltpu.VMEM((16, CH), BF16),
+            pltpu.VMEM((4, 16, CH), BF16),
+            pltpu.VMEM((16, CH), BF16),
+            pltpu.VMEM((8, 16, CH), BF16),
+            pltpu.VMEM((PER, 16, RES), BF16),
+            pltpu.VMEM((PER, RES, RES), BF16),
+            pltpu.VMEM((PER, 16, RES), BF16),
+            pltpu.VMEM((PER, 16, RES), BF16),
             pltpu.VMEM((2, 6 * CH, CH), BF16),
             pltpu.VMEM((2, CH, CELLS), F32),
             pltpu.VMEM((2, 4, CH, CELLS), F32),

time: 138 us -> 129 us (0.935); the launches traced: 138 us -> 127 us
  Pallas kernels: 135 us -> 125 us
    pallas_call x1, Pallas kernels: 134 us -> 123 us  [on_device(): pl.pallas_call(kernel, out_shape=[jax.ShapeDtypeStruct((CELLS, CH), BF16)...]
where the time goes in v4:
time: 129 us; the launch traced here: 127 us
  Pallas kernels  125 us (97%)
  local copies, waits for them, and re-layouts  1.93 us (1%)
    pallas_call x1, Pallas kernels, on_device(): pl.pallas_call(kernel, out_shape=[jax.ShapeDtypeStruct((CELLS, CH), BF16)...  123 us

profile of v4, /device:TPU:24, one launch (start us, length us, event | category | flops | bytes accessed | tf_op | source)
XLA Modules:
  0.0 127.5 jit_solution(5201021783269457912)
XLA Ops:
  0.6 0.0 copy-start
  0.6 1.0 copy.19
  1.6 0.0 copy-done
  1.6 0.0 copy-start.1
  1.6 0.0 copy-start.2
  1.7 0.0 copy-start.3
  1.7 0.0 copy-start.4
  1.7 0.0 copy-start.5
  1.7 0.0 copy-start.6
  1.7 0.1 copy.17
  1.8 0.8 copy-done.1
  2.6 0.0 copy-done.2
  2.6 0.0 copy-done.3
  2.6 0.0 copy-done.4
  2.6 0.0 copy-done.5
  2.6 0.0 copy-done.6
  2.6 123.4 %evoformer.1 = (bf16[128,128]{1,0:T(8,128)(2,1)S(1)}, f32[2,128,256]{2,1,0:T(8,128)S(1)}, f32[128,128]{1,0:T(8,128)S(1)}, f32[64,256]{1,0:T(8,128)S(1)}, bf16[10...) custom-call(bf16[2,128,256]{2,1,0:T(8,128)(2,1)S(1)} %bitcast.15, bf16[128,128]{1,0:T(8,128)(2,1)S(1)} %bitcast.16, ...), custom_call_target="tpu_custom_call" | custom-call | tf_op jit(solution)/shard_map/evoformer/pallas_call | solution.py:515
  126.0 1.5 %finish.1 = (bf16[128,128]{1,0:T(8,128)(2,1)}, f32[128,2,256]{2,1,0:T(2,128)}, f32[128,128]{1,0:T(8,128)}, f32[64,256]{1,0:T(8,128)}, f32[1024,128]{1,0:T(8,128)...) custom-call(bf16[128,128]{1,0:T(8,128)(2,1)S(1)} %get-tuple-element.22.updated_ref, ...), custom_call_target="tpu_custom_call" | custom-call | tf_op jit(solution)/shard_map/finish/pallas_call | solution.py:584
Async XLA Ops:
  0.6 1.0 copy-start
  1.6 0.9 copy-start.1
  1.6 1.0 copy-start.2
  1.7 1.0 copy-start.3
  1.7 1.0 copy-start.4
  1.7 0.9 copy-start.5
  1.7 0.9 copy-start.6

commit v5 on v4

--- a/solution.py
+++ b/solution.py
@@ -61,7 +61,7 @@
     cot_send, cot_recv,
     outer_send, outer_near, outer_part, outer_far, outer_own, outer_all,
     left0_chan, right0_chan, left1_chan, right1_chan, triangle_t, normed_s, parts_s, gate_s, tail_s, logit_s, upstream_s,
-    early_send, early_near, early_class, early_far, early_own, early_all,
+    early_send, early_near, early_class, early_far, early_own,
     late_send, late_near, late_class, late_far, late_own, late_all,
     send_sem, recv_sem,
 ):
@@ -180,7 +180,6 @@
 
     rights = lambda g, e: right_all.at[:, g, e]
     lefts = lambda g, e: left_all.at[:, g, e]
-    earlies = lambda g, e: early_all.at[g, e]
     lates = lambda g, e: late_all.at[g, e]
 
     barrier = pltpu.get_barrier_semaphore()
@@ -300,7 +299,6 @@
     factor1_send[:, 0] = left_factor
     factor1_send[:, 1] = right_factor
     exchange_near(factor1_send, factor1_recv, 5)
-    forward_block(lefts, group, 1)
     gate(1)
     near_arrived(factor1_recv, 5)
     open_wide(wide_a, factor1_recv[:, 0], 8)
@@ -312,6 +310,7 @@
         put_channel(wide_c, mul(left_k, right_k, TN), k, DEVICES)
     mixed1_send[...] = close_wide(wide_c, DEVICES)
     exchange(mixed1_send, mixed1_recv, 6)
+    forward_block(lefts, group, 1)
     arrived(mixed1_recv, 6)
     pair = tail(1, pair, sum_groups(mixed1_recv))
     updated_ref[...] = mul(order, pair.astype(BF16), NT).astype(BF16)
@@ -348,6 +347,9 @@
     upstream = upstream_s[0]
     update_grad, back1_send[...] = tail_back(1, upstream)
     exchange_global(back1_send, back1_recv, 7)
+    forward_arrived(lefts, 1, 27, 1)
+    forward_arrived(lefts, 2, 27, 1)
+    forward_arrived(lefts, 0, 27, 1)
     early = tail_weights(1, upstream, update_grad)
     arrived(back1_recv, 7)
     open_wide(wide_a, back1_recv[...], DEVICES)
@@ -358,14 +360,11 @@
     grad1_send[:, 0] = close_wide(wide_b, 8)
     grad1_send[:, 1] = close_wide(wide_c, 8)
     exchange_near(grad1_send, grad1_recv, 8)
-    forward_arrived(lefts, 1, 27, 1)
-    forward_arrived(lefts, 2, 27, 1)
     near_arrived(grad1_recv, 8)
     quarter, upstream = head_back(1, upstream, whole(grad1_recv[:, 0]), whole(grad1_recv[:, 1]))
 
     update_grad, back0_send[...] = tail_back(0, upstream)
     exchange_near(back0_send, back0_recv, 9)
-    forward_arrived(lefts, 0, 27, 1)
     early += head_weights(1, quarter)
     early += tail_weights(0, upstream, update_grad)
     early_send[...] = jnp.concatenate(early, axis=0).reshape(GRID + (EARLY, CH))
@@ -398,8 +397,8 @@
     exchange(cot_send, cot_recv, 10)
     for k in range(4):
         pair_grad_ref[pl.ds((k // 2) * RES + k % 2, DEVICES, stride=2), :] = cells[k * DEVICES : (k + 1) * DEVICES]
-    scatter_sum(early_far, early_own, early_all, 14)
-    gather_far(early_own, earlies, 34)
+    received(early_far.at[pl.ds(1, 3)], 14)
+    early_own[...] = jnp.sum(early_far[...].astype(F32), axis=0).astype(BF16)
 
     def factor_grad(cot, weight, factors):
         wide = (mul(cot, weight, NT) * (1.0 / SEQ)).astype(BF16).astype(F32)
@@ -429,9 +428,10 @@
         back = mul(grads[j], outer_ref[...], TN)
         alignment_grad_ref[j] = norm_back(aligned[j], aligned_inv[j], back, 1)
 
-    far_received(earlies, 34)
-    gather_near(earlies, 15)
-    scatter_sum(late_far, late_own, late_all, 17)
+    received(late_far.at[pl.ds(1, 3)], 17)
+    late_own[:EARLY] = early_own[...]
+    late_own[EARLY:] = jnp.sum(late_far[...].astype(F32), axis=0).astype(BF16)
+    late_all[group, place] = late_own[...]
     gather_far(late_own, lates, 41)
     near_arrived(outer_near, 11)
     total = jnp.sum(outer_near[...].astype(F32), axis=0).astype(BF16)
@@ -447,8 +447,6 @@
         remote(outer_own, outer_all.at[place], 46, peer).start()
     outer_all[place] = total
 
-    near_received(earlies, 15)
-    early_ref[...] = early_all[...].reshape(DEVICES * EARLY, CH)
 
     gather_left(rights, 20, 0)
     gather_left(lefts, 27, 1)
@@ -467,7 +465,6 @@
     left(outer_far.at[pl.ds(0, 3)], 12)
     near_sent(outer_all, 46)
     scatter_left(early_near, early_far, 13, 14)
-    gather_left(earlies, 34, 15)
     scatter_left(late_near, late_far, 16, 17)
 
     near_arrived(outer_all, 46)
@@ -475,7 +472,8 @@
     outer_grad_ref[:, :CH] = outer[: 2 * OUT]
     outer_grad_ref[:, CH:] = outer[2 * OUT :]
     near_received(lates, 18)
-    late_ref[...] = late_all[...].reshape(DEVICES * LATE, CH)
+    early_ref[...] = late_all[:, :, :EARLY].reshape(DEVICES * EARLY, CH)
+    late_ref[...] = late_all[:, :, EARLY:].reshape(DEVICES * LATE, CH)
     gather_left(lates, 41, 18)
 
 
@@ -560,8 +558,10 @@
             pltpu.VMEM((2, 3, CH, CELLS), F32),
             pltpu.VMEM((2, CH, CELLS), BF16),
             pltpu.VMEM((2, CH, CELLS), F32),
-            *sums(EARLY),
-            *sums(LATE),
+            *sums(EARLY)[:5],
+            *sums(LATE)[:4],
+            pltpu.VMEM((EARLY + LATE, CH), BF16),
+            pltpu.VMEM(GRID + (EARLY + LATE, CH), BF16),
             pltpu.SemaphoreType.DMA((48,)),
             pltpu.SemaphoreType.DMA((48,)),
         ],

time: 129 us -> 126 us (0.977)
  Pallas kernels: 125 us -> 123 us
    pallas_call x1, Pallas kernels: 123 us -> 121 us  [on_device(): pl.pallas_call(kernel, out_shape=[jax.ShapeDtypeStruct((CELLS, CH), BF16)...]
where the time goes in v5:
time: 126 us
  Pallas kernels  123 us (98%)
  local copies, waits for them, and re-layouts  1.93 us (2%)
    pallas_call x1, Pallas kernels, on_device(): pl.pallas_call(kernel, out_shape=[jax.ShapeDtypeStruct((CELLS, CH), BF16)...  121 us

profile of v5, /device:TPU:24, one launch (start us, length us, event | category | flops | bytes accessed | tf_op | source)
XLA Modules:
  0.0 125.5 jit_solution(3424072191801747190)
XLA Ops:
  0.6 0.0 copy-start
  0.6 1.0 copy.19
  1.6 0.0 copy-done
  1.6 0.0 copy-start.1
  1.6 0.0 copy-start.2
  1.7 0.0 copy-start.3
  1.7 0.0 copy-start.4
  1.7 0.0 copy-start.5
  1.7 0.0 copy-start.6
  1.7 0.1 copy.17
  1.8 0.8 copy-done.1
  2.6 0.0 copy-done.2
  2.6 0.0 copy-done.3
  2.6 0.0 copy-done.4
  2.6 0.0 copy-done.5
  2.6 0.0 copy-done.6
  2.6 121.4 %evoformer.1 = (bf16[128,128]{1,0:T(8,128)(2,1)S(1)}, f32[2,128,256]{2,1,0:T(8,128)S(1)}, f32[128,128]{1,0:T(8,128)S(1)}, f32[64,256]{1,0:T(8,128)S(1)}, bf16[10...) custom-call(bf16[2,128,256]{2,1,0:T(8,128)(2,1)S(1)} %bitcast.15, bf16[128,128]{1,0:T(8,128)(2,1)S(1)} %bitcast.16, ...), custom_call_target="tpu_custom_call" | custom-call | tf_op jit(solution)/shard_map/evoformer/pallas_call | solution.py:513
  124.1 1.5 %finish.1 = (bf16[128,128]{1,0:T(8,128)(2,1)}, f32[128,2,256]{2,1,0:T(2,128)}, f32[128,128]{1,0:T(8,128)}, f32[64,256]{1,0:T(8,128)}, f32[1024,128]{1,0:T(8,128)...) custom-call(bf16[128,128]{1,0:T(8,128)(2,1)S(1)} %get-tuple-element.22.updated_ref, ...), custom_call_target="tpu_custom_call" | custom-call | tf_op jit(solution)/shard_map/finish/pallas_call | solution.py:584
Async XLA Ops:
  0.6 1.0 copy-start
  1.6 0.9 copy-start.1
  1.6 1.0 copy-start.2
  1.7 1.0 copy-start.3
  1.7 1.0 copy-start.4
  1.7 0.9 copy-start.5
  1.7 0.9 copy-start.6

commit v6 on v5

--- a/solution.py
+++ b/solution.py
@@ -141,7 +141,6 @@
         forward_block(whole, far_source[k], phase)
 
     def gather_forward(whole, far_phase, phase):
-        forward_block(whole, group, phase)
         for k in reversed(range(len(FAR))):
             forward_arrived(whole, k, far_phase, phase)
 
@@ -196,6 +195,7 @@
 
     gather_far(right_own, rights, 20)
     right_all[:, group, place] = right_own[...]
+    forward_block(rights, group, 0)
     left_all[:, group, place] = left_own[...]
 
     row = lax.broadcasted_iota(jnp.int32, (CELLS, CELLS), 0)
@@ -433,6 +433,7 @@
     late_own[EARLY:] = jnp.sum(late_far[...].astype(F32), axis=0).astype(BF16)
     late_all[group, place] = late_own[...]
     gather_far(late_own, lates, 41)
+    forward_block(lates, group, 18)
     near_arrived(outer_near, 11)
     total = jnp.sum(outer_near[...].astype(F32), axis=0).astype(BF16)
     outer_part[...] = total

time: 126 us -> 126 us (level)
  no operation moved by 1% of the time
where the time goes in v6:
time: 126 us; the launch traced here: 125 us
  Pallas kernels  122 us (97%)
  local copies, waits for them, and re-layouts  1.93 us (2%)
    pallas_call x1, Pallas kernels, on_device(): pl.pallas_call(kernel, out_shape=[jax.ShapeDtypeStruct((CELLS, CH), BF16)...  121 us

profile of v6, /device:TPU:24, one launch (start us, length us, event | category | flops | bytes accessed | tf_op | source)
XLA Modules:
  0.0 125.1 jit_solution(10829227697084674228)
XLA Ops:
  0.6 0.0 copy-start
  0.6 1.0 copy.19
  1.6 0.0 copy-done
  1.6 0.0 copy-start.1
  1.6 0.0 copy-start.2
  1.7 0.0 copy-start.3
  1.7 0.0 copy-start.4
  1.7 0.0 copy-start.5
  1.7 0.0 copy-start.6
  1.7 0.1 copy.17
  1.8 0.8 copy-done.1
  2.6 0.0 copy-done.2
  2.6 0.0 copy-done.3
  2.6 0.0 copy-done.4
  2.6 0.0 copy-done.5
  2.6 0.0 copy-done.6
  2.6 121.0 %evoformer.1 = (bf16[128,128]{1,0:T(8,128)(2,1)S(1)}, f32[2,128,256]{2,1,0:T(8,128)S(1)}, f32[128,128]{1,0:T(8,128)S(1)}, f32[64,256]{1,0:T(8,128)S(1)}, bf16[10...) custom-call(bf16[2,128,256]{2,1,0:T(8,128)(2,1)S(1)} %bitcast.15, bf16[128,128]{1,0:T(8,128)(2,1)S(1)} %bitcast.16, ...), custom_call_target="tpu_custom_call" | custom-call | tf_op jit(solution)/shard_map/evoformer/pallas_call | solution.py:514
  123.6 1.5 %finish.1 = (bf16[128,128]{1,0:T(8,128)(2,1)}, f32[128,2,256]{2,1,0:T(2,128)}, f32[128,128]{1,0:T(8,128)}, f32[64,256]{1,0:T(8,128)}, f32[1024,128]{1,0:T(8,128)...) custom-call(bf16[128,128]{1,0:T(8,128)(2,1)S(1)} %get-tuple-element.22.updated_ref, ...), custom_call_target="tpu_custom_call" | custom-call | tf_op jit(solution)/shard_map/finish/pallas_call | solution.py:585
Async XLA Ops:
  0.6 1.0 copy-start
  1.6 0.9 copy-start.1
  1.6 1.0 copy-start.2
  1.7 1.0 copy-start.3
  1.7 1.0 copy-start.4
  1.7 0.9 copy-start.5
  1.7 0.9 copy-start.6
